TPU v7x, 32 devices: a whole 2x2x4 slice. The times are simulated.
32 devices in a mesh: outer: 8 (over y, x, core), inner: 4 (over z).
Axes of the slice: x: 2, y: 2, z: 4, core: 2. Of those that a mesh axis runs over, the one named last changes fastest.
Arguments:
- photo_embedding_matrix: bfloat16 [4096, 1152], P(('outer', 'inner')), may hold values from -1 to 1
- sentence_embedding_matrix: bfloat16 [4096, 1152], P(('outer', 'inner')), may hold values from -1 to 1
- logit_stretch_factor: float32 [1], replicated, may hold values from 4 to 8
- logit_offset_term: float32 [1], replicated, may hold values from -4 to -2
Outputs:
- grad_image: float32 [4096, 1152], P(('outer', 'inner'))
- grad_text: float32 [4096, 1152], P(('outer', 'inner'))
All inputs are finite; a program needn't handle non-finite values.
Results may differ from a plain program's by a relative error of at most 0.0027.
Values may be sent and summed in bfloat16 or wider, within the bound.
A program may use at most 64 MiB of HBM per device.

v0:
```python
import jax
import jax.numpy as jnp
from jax import lax
from jax.sharding import PartitionSpec as P


def shifted(block, axis, distance):
    devices = range(lax.axis_size(axis))
    route = [((i - distance) % len(devices), i) for i in devices]
    return lax.ppermute(block, axis, route)


def signed_multiplier(left_rows, right_rows, reciprocal_logit_temp, offset, positive):
    scores = (
        reciprocal_logit_temp
        * lax.dot_general(
            left_rows, right_rows, (((1,), (1,)), ((), ())), preferred_element_type=jnp.float32
        )
        + offset
    )
    signs = jnp.where(positive, 1.0, -1.0).astype(jnp.float32)
    return (-signs * jax.nn.sigmoid(-signs * scores) * reciprocal_logit_temp).astype(jnp.bfloat16)


def per_device(
    photo_embedding_matrix, sentence_embedding_matrix, logit_stretch_factor, logit_offset_term
):
    row_count = photo_embedding_matrix.shape[0]
    reciprocal_logit_temp = logit_stretch_factor[0]
    offset = logit_offset_term[0]
    group_text = lax.all_gather(sentence_embedding_matrix, "inner", axis=0, tiled=True)
    visiting_partner_blocks = shifted(photo_embedding_matrix, "outer", -1)
    block_rows = group_text.shape[0]
    leading_row_index = lax.axis_index("inner") * row_count
    row_index = lax.broadcasted_iota(jnp.int32, (row_count, block_rows), 0)
    column_position = lax.broadcasted_iota(jnp.int32, (row_count, block_rows), 1)
    positive = column_position == row_index + leading_row_index
    nothing = column_position < 0
    own_coef = signed_multiplier(
        photo_embedding_matrix, group_text, reciprocal_logit_temp, offset, positive
    )
    guest_coef = signed_multiplier(
        visiting_partner_blocks, group_text, reciprocal_logit_temp, offset, nothing
    )
    own_grad = jnp.dot(own_coef, group_text, preferred_element_type=jnp.float32)
    guest_grad = jnp.dot(guest_coef, group_text, preferred_element_type=jnp.float32)
    grad_image = own_grad + shifted(guest_grad, "outer", 1)
    partial_value = lax.dot_general(
        own_coef,
        photo_embedding_matrix,
        (((0,), (0,)), ((), ())),
        preferred_element_type=jnp.float32,
    )
    grad_text = lax.psum_scatter(
        partial_value
        + lax.dot_general(
            guest_coef,
            visiting_partner_blocks,
            (((0,), (0,)), ((), ())),
            preferred_element_type=jnp.float32,
        ),
        "inner",
        scatter_dimension=0,
        tiled=True,
    )
    return (grad_image, grad_text)


def solution(mesh):
    return jax.shard_map(
        per_device,
        mesh=mesh,
        in_specs=(P(("outer", "inner"), None), P(("outer", "inner"), None), P(), P()),
        out_specs=(P(("outer", "inner"), None), P(("outer", "inner"), None)),
        check_vma=False,
    )
```

profile of v0, /device:TPU:0, one launch (start us, length us, event | category | flops | bytes accessed | tf_op | source)
XLA Modules:
  0.0 102.7 jit_solution(18278691674384884066)
XLA Ops:
  7.2 0.0 all-gather.2.cloned.1.call-start
  7.2 0.7 all-gather.2.cloned.1.call-update
  7.9 0.0 reduce-scatter.2.cloned.1.call-start
  7.9 3.4 %collective-permute-start = (bf16[128,1152]{1,0:T(8,128)(2,1)}, bf16[128,1152]{1,0:T(8,128)(2,1)S(1)}, u32[]{:S(2)}, u32[]{:S(2)}) collective-permute-start(bf16[128,1152]{1,0:T(8,128)(2,1)} %param.4), channel_id=1, source_target_pairs={{4,0},{8,4},{12,8},{16,12},{20,16},{24,20},{28,24},{0,28},{5,1},{9... | collective-permute-start | bytes 884744 | tf_op jit(solution)/shard_map/ppermute | solution.py:10
  12.6 30.1 %all-gather.2.cloned.1.call-done = bf16[512,1152]{1,0:T(8,128)(2,1)} async-done(((bf16[128,1152]{1,0:T(8,128)(2,1)}), bf16[512,1152]{1,0:T(8,128)(2,1)}) %all-gather.2.cloned.1.call-update) | async-done | bytes 1179664 | tf_op jit(solution)/shard_map/all_gather | solution.py:31
  42.7 0.0 copy-start.1
  42.7 2.0 %fusion.14 = bf16[128,512]{1,0:T(8,128)(2,1)S(1)} fusion(bf16[128,1152]{1,0:T(8,128)(2,1)} %param.4, bf16[512,1152]{1,0:T(8,128)(2,1)} %all-gather.2.cloned.1.call-done, f32[]{:T(128)} %bitcast.16, f32[]{:T(128)} %bitcast.15, s32[128]{0:T(128)S(1)} %iota_add_fusion), kind=kOutput, calls=%fused_computation.18 | convolution fusion | flops 151781376 | bytes 1606152 | tf_op jit(solution)/shard_map/dot_general | solution.py:16
  44.7 0.0 copy-done.1
  44.8 0.0 copy-start
  44.8 0.5 fusion.17
  45.3 0.0 collective-permute-done
  45.3 0.8 copy-done
  46.0 0.6 fusion.15
  46.6 1.9 %convolution_add_fusion = f32[512,1152]{1,0:T(8,128)} fusion(f32[512,1152]{1,0:T(8,128)S(1)} %fusion.17, bf16[128,512]{1,0:T(8,128)(2,1)S(1)} %fusion.15, bf16[128,1152]{1,0:T(8,128)(2,1)S(1)} %collective-permute-done), kind=kOutput, calls=%fused_computation | convolution fusion | flops 151584768 | bytes 5144576 | tf_op jit(solution)/shard_map/dot_general | solution.py:56
  48.5 0.0 reduce-scatter.2.cloned.1.call-update
  48.5 0.3 fusion.16
  48.9 0.1 collective-permute-start.1
  48.9 10.2 %collective-permute-done.1 = f32[128,1152]{1,0:T(8,128)S(1)} collective-permute-done((f32[128,1152]{1,0:T(8,128)S(1)}, f32[128,1152]{1,0:T(8,128)S(1)}, u32[]{:S(2)}, u32[]{:S(2)}) %collective-permute-start.1) | collective-permute-done | bytes 589856 | tf_op jit(solution)/shard_map/ppermute | solution.py:10
  59.1 1.2 %convolution_add_fusion.1 = f32[128,1152]{1,0:T(8,128)} fusion(f32[128,1152]{1,0:T(8,128)S(1)} %collective-permute-done.1, bf16[128,512]{1,0:T(8,128)(2,1)S(1)} %fusion.14, bf16[512,1152]{1,0:T(8,128)(2,1)S(1)} %copy-done), kind=kOutput, calls=%fused_computation.1 | convolution fusion | flops 151142400 | bytes 2490368 | tf_op jit(solution)/shard_map/dot_general | solution.py:45
  60.3 35.5 %reduce-scatter.2.cloned.1.call-done = f32[128,1152]{1,0:T(8,128)} async-done(((f32[512,1152]{1,0:T(8,128)}), f32[128,1152]{1,0:T(8,128)}) %reduce-scatter.2.cloned.1.call-update) | async-done | bytes 589840 | tf_op jit(solution)/shard_map/reduce_scatter | solution.py:54
  (1 shorter events, 0.0 us)
Async XLA Ops:
  7.2 35.6 %all-gather.2.cloned.1.call-start = ((), (), s32[]{:S(2)}) async-start(), calls=%async_computation.1 | async-start | bytes 1474560 | tf_op jit(solution)/shard_map/all_gather | solution.py:31
  7.9 87.9 %reduce-scatter.2.cloned.1.call-start = ((), (), s32[]{:S(2)}) async-start(), calls=%async_computation.2 | async-start | bytes 2949120 | tf_op jit(solution)/shard_map/reduce_scatter | solution.py:54
  7.9 37.3 %collective-permute-start = (bf16[128,1152]{1,0:T(8,128)(2,1)}, bf16[128,1152]{1,0:T(8,128)(2,1)S(1)}, u32[]{:S(2)}, u32[]{:S(2)}) collective-permute-start(bf16[128,1152]{1,0:T(8,128)(2,1)} %param.4), channel_id=1, source_target_pairs={{4,0},{8,4},{12,8},{16,12},{20,16},{24,20},{28,24},{0,28},{5,1},{9... | collective-permute-start | bytes 884744 | tf_op jit(solution)/shard_map/ppermute | solution.py:10
  42.7 2.0 %copy-start.1 = (bf16[128,1152]{1,0:T(8,128)(2,1)S(1)}, bf16[128,1152]{1,0:T(8,128)(2,1)}, u32[]{:S(2)}) copy-start(bf16[128,1152]{1,0:T(8,128)(2,1)} %param.4) | copy-start | bytes 884740
  44.8 1.3 %copy-start = (bf16[512,1152]{1,0:T(8,128)(2,1)S(1)}, bf16[512,1152]{1,0:T(8,128)(2,1)}, u32[]{:S(2)}) copy-start(bf16[512,1152]{1,0:T(8,128)(2,1)} %all-gather.2.cloned.1.call-done) | copy-start | bytes 3538948
  48.9 10.3 %collective-permute-start.1 = (f32[128,1152]{1,0:T(8,128)S(1)}, f32[128,1152]{1,0:T(8,128)S(1)}, u32[]{:S(2)}, u32[]{:S(2)}) collective-permute-start(f32[128,1152]{1,0:T(8,128)S(1)} %fusion.16), channel_id=1, source_target_pairs={{28,0},{0,4},{4,8},{8,12},{12,16},{16,20},{20,24},{24,28},{29,1},{... | collective-permute-start | bytes 1769480 | tf_op jit(solution)/shard_map/ppermute | solution.py:10
Sparse Core Ops, SparseCore 0:
  9.6 33.1 all-gather.1
  48.6 47.1 reduce-scatter.1
where the time goes:
time: 103 us
  waiting for transfers between devices  76.5 us (74%)
  between operations  15.4 us (15%)
  matrix products  6.46 us (6%)
  starting transfers between devices  3.52 us (3%)
    reduce_scatter x1, waiting for transfers between devices, per_device(): lax.psum_scatter(partial_value + lax.dot_general(guest_coef, visiting_par...  35.5 us
    all_gather x1, waiting for transfers between devices, per_device(): lax.all_gather(sentence_embedding_matrix, 'inner', axis=0, tiled=True)  30.1 us
    ppermute x2, waiting for transfers between devices, shifted(): return lax.ppermute(block, axis, route)  10.2 us
    ppermute x2, starting transfers between devices, shifted(): return lax.ppermute(block, axis, route)  3.44 us
    dot_general x2, matrix products, signed_multiplier(): lax.dot_general(left_rows, right_rows, (((1,), (1,)), ((), ())), preferre...  2.56 us
  transfers between devices with their start and end apart: 4, of which 3 were waited for; matrix products, arithmetic and copies ran while one was open for 4% of the time, Pallas kernels for 0%

commit v1 on v0

v1 whole, which is shorter than its diff:
```python
import functools

import jax
import jax.numpy as jnp
from jax import lax
from jax.experimental import pallas as pl
from jax.experimental.pallas import tpu as pltpu
from jax.sharding import PartitionSpec as P

MESH = pl.DeviceIdType.MESH
TEXT, IMAGE = 0, 1


def kernel(
    n, m, image, text, scale, offset, grad_image, grad_text,
    own, group, guest, load_sem, line_send, line_recv, side_send, side_recv,
):
    outer, z = lax.axis_index("outer"), lax.axis_index("inner")
    above, below = lax.rem(outer + 1, m), lax.rem(outer + m - 1, m)
    rows = text.shape[0]
    source = (text, image)
    side = (above, below)

    loads = [pltpu.make_async_copy(source[k], own.at[k], load_sem.at[k]) for k in (TEXT, IMAGE)]
    for load in loads:
        load.start()

    barrier = pltpu.get_barrier_semaphore()

    def greet(o, i):
        pl.semaphore_signal(barrier, inc=1, device_id=(o, i), device_id_type=MESH)

    greet(above, z)
    greet(below, z)
    pl.when(z > 0)(lambda: greet(outer, z - 1))
    pl.when(z < n - 1)(lambda: greet(outer, z + 1))
    pl.semaphore_wait(barrier, 2 + (z > 0).astype(jnp.int32) + (z < n - 1).astype(jnp.int32))

    def along(k, src, slot, way):
        return pltpu.make_async_remote_copy(
            src_ref=src,
            dst_ref=group.at[k, slot],
            send_sem=line_send.at[k, slot, way],
            recv_sem=line_recv.at[k, slot],
            device_id=(outer, z + (1 if way else -1)),
            device_id_type=MESH,
        )

    def across(k, src, slot):
        return pltpu.make_async_remote_copy(
            src_ref=src,
            dst_ref=guest.at[k, slot],
            send_sem=side_send.at[k, slot],
            recv_sem=side_recv.at[k, slot],
            device_id=(side[k], z),
            device_id_type=MESH,
        )

    def has_next(way):
        return z < n - 1 if way else z > 0

    def add(k, block, first=False):
        out = (grad_image, grad_text)[k]
        product = lax.dot_general(
            own[1 - k], block[...], (((1,), (1,)), ((), ())), preferred_element_type=jnp.float32
        )
        logit = scale[0] * product + offset[0]
        if first:
            row = lax.broadcasted_iota(jnp.int32, (rows, rows), 0)
            column = lax.broadcasted_iota(jnp.int32, (rows, rows), 1)
            sign = jnp.where(row == column, 1.0, -1.0)
            coef = -sign * jax.nn.sigmoid(-sign * logit) * scale[0]
        else:
            coef = jax.nn.sigmoid(logit) * scale[0]
        term = jnp.dot(coef.astype(jnp.bfloat16), block[...], preferred_element_type=jnp.float32)
        out[...] = term if first else out[...] + term

    for k in (TEXT, IMAGE):
        for way in (1, 0):
            pl.when(has_next(way))(lambda: along(k, source[k], z, way).start())
        across(k, source[k], z).start()

    for load in loads:
        load.wait()
    for k in (TEXT, IMAGE):
        add(k, own.at[k], first=True)

    def visit(k, slot):
        across(k, guest.at[k, slot], slot).wait_recv()
        add(k, guest.at[k, slot])

    visit(TEXT, z)

    def step(s, _):
        def from_line(k):
            for way in (1, 0):
                slot = z - s if way else z + s

                @pl.when(slot >= 0 if way else slot < n)
                def _():
                    along(k, source[k], slot, way).wait_recv()
                    pl.when(has_next(way))(
                        lambda: along(k, group.at[k, slot], slot, way).start()
                    )
                    across(k, group.at[k, slot], slot).start()

            for way in (1, 0):
                slot = z - s if way else z + s
                pl.when(slot >= 0 if way else slot < n)(lambda: add(k, group.at[k, slot]))

        from_line(TEXT)
        pl.when(z - s + 1 >= 0)(lambda: visit(IMAGE, z - s + 1))
        pl.when((z + s - 1 < n) & (s > 1))(lambda: visit(IMAGE, z + s - 1))
        from_line(IMAGE)
        pl.when(z - s >= 0)(lambda: visit(TEXT, z - s))
        pl.when(z + s < n)(lambda: visit(TEXT, z + s))
        return 0

    lax.fori_loop(1, n, step, 0)
    if n > 1:
        pl.when(z - n + 1 >= 0)(lambda: visit(IMAGE, z - n + 1))
        pl.when(z + n - 1 < n)(lambda: visit(IMAGE, z + n - 1))

    def drain(slot, _):
        for k in (TEXT, IMAGE):
            across(k, source[k], slot).wait_send()
            pl.when((slot <= z) & (z < n - 1))(lambda: along(k, source[k], slot, 1).wait_send())
            pl.when((slot >= z) & (z > 0))(lambda: along(k, source[k], slot, 0).wait_send())
        return 0

    lax.fori_loop(0, n, drain, 0)


def solution(mesh):
    n, m = mesh.shape["inner"], mesh.shape["outer"]

    def per_device(image, text, scale, offset):
        rows, width = image.shape
        dma = pltpu.SemaphoreType.DMA
        return pl.pallas_call(
            functools.partial(kernel, n, m),
            out_shape=(jax.ShapeDtypeStruct((rows, width), jnp.float32),) * 2,
            in_specs=[pl.BlockSpec(memory_space=pl.ANY)] * 2
            + [pl.BlockSpec(memory_space=pltpu.SMEM)] * 2,
            out_specs=(pl.BlockSpec(memory_space=pltpu.VMEM),) * 2,
            scratch_shapes=[
                pltpu.VMEM((2, rows, width), jnp.bfloat16),
                pltpu.VMEM((2, n, rows, width), jnp.bfloat16),
                pltpu.VMEM((2, n, rows, width), jnp.bfloat16),
                dma((2,)),
                dma((2, n, 2)),
                dma((2, n)),
                dma((2, n)),
                dma((2, n)),
            ],
            compiler_params=pltpu.CompilerParams(
                collective_id=0, has_side_effects=True, vmem_limit_bytes=32 * 1024 * 1024
            ),
            cost_estimate=pl.CostEstimate(
                flops=16 * n * rows * rows * width,
                bytes_accessed=12 * rows * width,
                transcendentals=4 * n * rows * rows,
            ),
        )(image, text, scale, offset)

    return jax.shard_map(
        per_device,
        mesh=mesh,
        in_specs=(P(("outer", "inner"), None), P(("outer", "inner"), None), P(), P()),
        out_specs=(P(("outer", "inner"), None), P(("outer", "inner"), None)),
        check_vma=False,
    )
```

time: 103 us -> 55.7 us (0.54)
  the two profiles are of different devices: /device:TPU:0 before, /device:TPU:1 now
where the time goes in v1:
time: 55.7 us; the launch traced here: 55.5 us
  Pallas kernels  50 us (90%)
  local copies, waits for them, and re-layouts  3.55 us (6%)
  between operations  1.94 us (3%)
    pallas_call x1, Pallas kernels, per_device(): pl.pallas_call(functools.partial(kernel, n, m), out_shape=(jax.ShapeDtype...  50 us
    unnamed x6, local copies, waits for them, and re-layouts  3.55 us

profile of v1, /device:TPU:1, one launch (start us, length us, event | category | flops | bytes accessed | tf_op | source)
XLA Modules:
  0.0 55.5 jit_solution(15790696263802020140)
XLA Ops:
  1.9 0.0 copy-start
  1.9 1.0 %copy-done = bf16[128,1152]{1,0:T(8,128)(2,1)S(1)} copy-done((bf16[128,1152]{1,0:T(8,128)(2,1)S(1)}, bf16[128,1152]{1,0:T(8,128)(2,1)}, u32[]{:S(2)}) %copy-start) | copy-done | bytes 294936
  2.9 0.0 copy-start.1
  2.9 1.0 %copy-done.1 = bf16[128,1152]{1,0:T(8,128)(2,1)S(1)} copy-done((bf16[128,1152]{1,0:T(8,128)(2,1)S(1)}, bf16[128,1152]{1,0:T(8,128)(2,1)}, u32[]{:S(2)}) %copy-start.1) | copy-done | bytes 294936
  3.8 50.0 %shard_map.59 = (f32[128,1152]{1,0:T(8,128)S(1)}, f32[128,1152]{1,0:T(8,128)S(1)}) custom-call(bf16[128,1152]{1,0:T(8,128)(2,1)S(1)} %copy-done, bf16[128,1152]{1,0:T(8,128)(2,1)S(1)} %copy-done.1, f32[1]{0:T(128)S(6)} %copy.8.scale, f32[1]{0:T(128)S(6)} %copy.9.offset), custom_call_target="tpu_custom_call" | custom-call | flops 1207959552 | bytes 1769472 | tf_op jit(solution)/shard_map/pallas_call | solution.py:140
  53.9 0.8 %copy.10 = f32[128,1152]{1,0:T(8,128)} copy(f32[128,1152]{1,0:T(8,128)S(1)} %get-tuple-element.4) | data formatting | bytes 1179648
  54.7 0.8 %copy.11 = f32[128,1152]{1,0:T(8,128)} copy(f32[128,1152]{1,0:T(8,128)S(1)} %get-tuple-element.5) | data formatting | bytes 1179648
Async XLA Ops:
  1.9 1.0 %copy-start = (bf16[128,1152]{1,0:T(8,128)(2,1)S(1)}, bf16[128,1152]{1,0:T(8,128)(2,1)}, u32[]{:S(2)}) copy-start(bf16[128,1152]{1,0:T(8,128)(2,1)} %image.1) | copy-start | bytes 884740
  2.9 1.0 %copy-start.1 = (bf16[128,1152]{1,0:T(8,128)(2,1)S(1)}, bf16[128,1152]{1,0:T(8,128)(2,1)}, u32[]{:S(2)}) copy-start(bf16[128,1152]{1,0:T(8,128)(2,1)} %text.1) | copy-start | bytes 884740

commit v2 on v1

--- a/solution.py
+++ b/solution.py
@@ -9,6 +9,7 @@
 
 MESH = pl.DeviceIdType.MESH
 TEXT, IMAGE = 0, 1
+HALVES = 2
 
 
 def kernel(
@@ -131,30 +132,240 @@
     lax.fori_loop(0, n, drain, 0)
 
 
+def line4_kernel(
+    m, image, text, scale, offset, grad_image, grad_text,
+    mine, group, guest, images, guest_images, total, part_out, part_in, row_out, row_in,
+    load_sem, line_send, line_recv, side_send, side_recv, image_send, image_recv,
+    guest_send, guest_recv, part_send, part_recv, row_send, row_recv,
+):
+    outer, z = lax.axis_index("outer"), lax.axis_index("inner")
+    above, below = lax.rem(outer + 1, m), lax.rem(outer + m - 1, m)
+    rows = text.shape[0]
+    half = rows // HALVES
+    is_end = (z == 0) | (z == 3)
+    is_middle = (z == 1) | (z == 2)
+    high = (z >= 2).astype(jnp.int32)
+    end, middle = 3 * high, 1 + high
+    far_end, far_middle = 3 - end, 3 - middle
+
+    loads = [
+        pltpu.make_async_copy(image, images.at[0], load_sem.at[0]),
+        pltpu.make_async_copy(text, mine, load_sem.at[1]),
+    ]
+    for load in loads:
+        load.start()
+
+    barrier = pltpu.get_barrier_semaphore()
+
+    def greet(o, i):
+        pl.semaphore_signal(barrier, inc=1, device_id=(o, i), device_id_type=MESH)
+
+    greet(above, z)
+    greet(below, z)
+    pl.when(z > 0)(lambda: greet(outer, z - 1))
+    pl.when(z < 3)(lambda: greet(outer, z + 1))
+    pl.semaphore_wait(barrier, 2 + (z > 0).astype(jnp.int32) + (z < 3).astype(jnp.int32))
+
+    def remote(src, dst, send, recv, o, i):
+        return pltpu.make_async_remote_copy(
+            src_ref=src, dst_ref=dst, send_sem=send, recv_sem=recv,
+            device_id=(o, i), device_id_type=MESH,
+        )
+
+    def along(src, slot, way, to):
+        return remote(src, group.at[slot], line_send.at[slot, way], line_recv.at[slot], outer, to)
+
+    def across(src, slot):
+        return remote(src, guest.at[slot], side_send.at[slot], side_recv.at[slot], above, z)
+
+    def image_inward():
+        return remote(image, images.at[1], image_send.at[0], image_recv.at[0], outer, middle)
+
+    def image_across(src, i):
+        return remote(src, guest_images.at[i], guest_send.at[i], guest_recv.at[i], below, z)
+
+    def part(i, h):
+        rows_h = pl.ds(h * half, half)
+        return remote(
+            part_out.at[i, rows_h], part_in.at[i, rows_h],
+            part_send.at[i, h], part_recv.at[i, h], outer, far_middle,
+        )
+
+    def row_block(h):
+        rows_h = pl.ds(h * half, half)
+        return remote(
+            row_out.at[rows_h], row_in.at[rows_h], row_send.at[h], row_recv.at[h], outer, end
+        )
+
+    def pair(left, right, positive):
+        product = lax.dot_general(
+            left, right[...], (((1,), (1,)), ((), ())), preferred_element_type=jnp.float32
+        )
+        logit = scale[0] * product + offset[0]
+        if positive:
+            row = lax.broadcasted_iota(jnp.int32, (rows, rows), 0)
+            column = lax.broadcasted_iota(jnp.int32, (rows, rows), 1)
+            sign = jnp.where(row == column, 1.0, -1.0)
+            coef = -sign * jax.nn.sigmoid(-sign * logit) * scale[0]
+        else:
+            coef = jax.nn.sigmoid(logit) * scale[0]
+        return jnp.dot(coef.astype(jnp.bfloat16), right[...], preferred_element_type=jnp.float32)
+
+    def add_image(block, positive=False, first=False):
+        term = pair(images[0], block, positive)
+        grad_image[...] = term if first else grad_image[...] + term
+
+    def add_text(i, left, block, positive=False, first=False):
+        term = pair(left[...], block, positive)
+        total[i] = term if first else total[i] + term
+
+    def arrive(slot):
+        along(text, slot, 0, end).wait_recv()
+
+    def visit(slot):
+        across(text, slot).wait_recv()
+        add_image(guest.at[slot])
+
+    @pl.when(is_end)
+    def _():
+        along(text, z, 0, middle).start()
+        image_inward().start()
+        across(text, z).start()
+        for load in loads:
+            load.wait()
+        add_image(mine, positive=True, first=True)
+        visit(z)
+        for slot, previous in ((middle, None), (far_middle, middle), (far_end, far_middle)):
+            arrive(slot)
+            across(group.at[slot], slot).start()
+            add_image(group.at[slot])
+            if previous is not None:
+                visit(previous)
+        visit(far_end)
+        for h in range(HALVES):
+            row_block(h).wait_recv()
+            rows_h = pl.ds(h * half, half)
+            grad_text[rows_h, :] = row_in[rows_h, :].astype(jnp.float32)
+        along(text, z, 0, middle).wait_send()
+        image_inward().wait_send()
+
+    @pl.when(is_middle)
+    def _():
+        along(text, z, 0, far_middle).start()
+        along(text, z, 1, end).start()
+        image_across(image, 0).start()
+        across(text, z).start()
+        for load in loads:
+            load.wait()
+        add_image(mine, positive=True, first=True)
+        add_text(0, mine, images.at[0], positive=True, first=True)
+        image_across(image, 0).wait_recv()
+        add_text(0, mine, guest_images.at[0])
+
+        arrive(end)
+        along(group.at[end], end, 0, far_middle).start()
+        across(group.at[end], end).start()
+        add_text(1, group.at[end], images.at[0], first=True)
+        arrive(far_middle)
+        along(group.at[far_middle], far_middle, 0, end).start()
+        across(group.at[far_middle], far_middle).start()
+        add_text(2, group.at[far_middle], images.at[0], first=True)
+        add_text(2, group.at[far_middle], guest_images.at[0])
+
+        image_inward().wait_recv()
+        image_across(images.at[1], 1).start()
+        arrive(far_end)
+        along(group.at[far_end], far_end, 0, end).start()
+        across(group.at[far_end], far_end).start()
+        add_text(3, group.at[far_end], images.at[0], first=True)
+        add_text(3, group.at[far_end], guest_images.at[0])
+        add_text(3, group.at[far_end], images.at[1])
+        add_text(2, group.at[far_middle], images.at[1])
+        image_across(image, 1).wait_recv()
+        for i, slot, to in ((3, far_end, 1), (2, far_middle, 0)):
+            add_text(i, group.at[slot], guest_images.at[1])
+            part_out[to] = total[i].astype(jnp.bfloat16)
+            for h in range(HALVES):
+                part(to, h).start()
+
+        add_text(1, group.at[end], guest_images.at[0])
+        add_text(1, group.at[end], images.at[1], positive=True)
+        add_text(1, group.at[end], guest_images.at[1])
+        for h in range(HALVES):
+            part(1, h).wait_recv()
+            rows_h = pl.ds(h * half, half)
+            row_out[rows_h, :] = (
+                total[1, rows_h, :] + part_in[1, rows_h, :].astype(jnp.float32)
+            ).astype(jnp.bfloat16)
+            row_block(h).start()
+        add_text(0, mine, images.at[1])
+        add_text(0, mine, guest_images.at[1])
+        for slot in (end, far_middle, far_end):
+            add_image(group.at[slot])
+        for slot in (z, end, far_middle, far_end):
+            visit(slot)
+        for h in range(HALVES):
+            part(0, h).wait_recv()
+            rows_h = pl.ds(h * half, half)
+            grad_text[rows_h, :] = total[0, rows_h, :] + part_in[0, rows_h, :].astype(jnp.float32)
+
+        along(text, z, 0, far_middle).wait_send()
+        along(text, z, 1, end).wait_send()
+        along(text, end, 0, far_middle).wait_send()
+        along(text, far_middle, 0, end).wait_send()
+        along(text, far_end, 0, end).wait_send()
+        for i in (0, 1):
+            image_across(image, i).wait_send()
+            for h in range(HALVES):
+                part(i, h).wait_send()
+        for h in range(HALVES):
+            row_block(h).wait_send()
+
+    for slot in range(4):
+        across(text, slot).wait_send()
+
+
 def solution(mesh):
     n, m = mesh.shape["inner"], mesh.shape["outer"]
 
     def per_device(image, text, scale, offset):
         rows, width = image.shape
         dma = pltpu.SemaphoreType.DMA
+        block = (rows, width)
+        if n == 4:
+            body = functools.partial(line4_kernel, m)
+            scratch = [
+                pltpu.VMEM(block, jnp.bfloat16),
+                pltpu.VMEM((4, *block), jnp.bfloat16),
+                pltpu.VMEM((4, *block), jnp.bfloat16),
+                pltpu.VMEM((2, *block), jnp.bfloat16),
+                pltpu.VMEM((2, *block), jnp.bfloat16),
+                pltpu.VMEM((4, *block), jnp.float32),
+                pltpu.VMEM((2, *block), jnp.bfloat16),
+                pltpu.VMEM((2, *block), jnp.bfloat16),
+                pltpu.VMEM(block, jnp.bfloat16),
+                pltpu.VMEM(block, jnp.bfloat16),
+                dma((2,)), dma((4, 2)), dma((4,)), dma((4,)), dma((4,)),
+                dma((1,)), dma((1,)), dma((2,)), dma((2,)),
+                dma((2, HALVES)), dma((2, HALVES)), dma((HALVES,)), dma((HALVES,)),
+            ]
+        else:
+            body = functools.partial(kernel, n, m)
+            scratch = [
+                pltpu.VMEM((2, *block), jnp.bfloat16),
+                pltpu.VMEM((2, n, *block), jnp.bfloat16),
+                pltpu.VMEM((2, n, *block), jnp.bfloat16),
+                dma((2,)), dma((2, n, 2)), dma((2, n)), dma((2, n)), dma((2, n)),
+            ]
         return pl.pallas_call(
-            functools.partial(kernel, n, m),
+            body,
             out_shape=(jax.ShapeDtypeStruct((rows, width), jnp.float32),) * 2,
             in_specs=[pl.BlockSpec(memory_space=pl.ANY)] * 2
             + [pl.BlockSpec(memory_space=pltpu.SMEM)] * 2,
             out_specs=(pl.BlockSpec(memory_space=pltpu.VMEM),) * 2,
-            scratch_shapes=[
-                pltpu.VMEM((2, rows, width), jnp.bfloat16),
-                pltpu.VMEM((2, n, rows, width), jnp.bfloat16),
-                pltpu.VMEM((2, n, rows, width), jnp.bfloat16),
-                dma((2,)),
-                dma((2, n, 2)),
-                dma((2, n)),
-                dma((2, n)),
-                dma((2, n)),
-            ],
+            scratch_shapes=scratch,
             compiler_params=pltpu.CompilerParams(
-                collective_id=0, has_side_effects=True, vmem_limit_bytes=32 * 1024 * 1024
+                collective_id=0, has_side_effects=True, vmem_limit_bytes=60 * 1024 * 1024
             ),
             cost_estimate=pl.CostEstimate(
                 flops=16 * n * rows * rows * width,

time: 55.7 us -> 44.1 us (0.79)
  Pallas kernels: 50 us -> 39.2 us
  local copies, waits for them, and re-layouts: 3.55 us -> 2.8 us
    pallas_call x1, Pallas kernels: 50 us -> 39.2 us  [per_device(): pl.pallas_call(body, out_shape=(jax.ShapeDtypeStruct((rows, width), jnp.f...]
    unnamed x6 -> x4, local copies, waits for them, and re-layouts: 3.55 us -> 2.8 us
where the time goes in v2:
time: 44.1 us; the launch traced here: 44 us
  Pallas kernels  39.2 us (89%)
  local copies, waits for them, and re-layouts  2.8 us (6%)
  between operations  1.94 us (4%)
    pallas_call x1, Pallas kernels, per_device(): pl.pallas_call(body, out_shape=(jax.ShapeDtypeStruct((rows, width), jnp.f...  39.2 us
    unnamed x4, local copies, waits for them, and re-layouts  2.8 us

profile of v2, /device:TPU:1, one launch (start us, length us, event | category | flops | bytes accessed | tf_op | source)
XLA Modules:
  0.0 44.0 jit_solution(15522551035291670287)
XLA Ops:
  1.9 39.2 %shard_map.59 = (f32[128,1152]{1,0:T(8,128)}, f32[128,1152]{1,0:T(8,128)}) custom-call(bf16[128,1152]{1,0:T(8,128)(2,1)} %image.1, bf16[128,1152]{1,0:T(8,128)(2,1)} %text.1, f32[1]{0:T(128)S(6)} %copy.8.scale, f32[1]{0:T(128)S(6)} %copy.9.offset), custom_call_target="tpu_custom_call" | custom-call | flops 1207959552 | bytes 1769472 | tf_op jit(solution)/shard_map/pallas_call | solution.py:360
  41.2 0.0 copy-start
  41.2 2.0 %copy.10 = f32[128,1152]{1,0:T(8,128)} copy(f32[128,1152]{1,0:T(8,128)} %get-tuple-element.4) | data formatting | bytes 1179648
  43.1 0.0 copy-done
  43.2 0.8 %copy.11 = f32[128,1152]{1,0:T(8,128)} copy(f32[128,1152]{1,0:T(8,128)S(1)} %copy-done) | data formatting | bytes 1179648
Async XLA Ops:
  41.2 2.0 %copy-start = (f32[128,1152]{1,0:T(8,128)S(1)}, f32[128,1152]{1,0:T(8,128)}, u32[]{:S(2)}) copy-start(f32[128,1152]{1,0:T(8,128)} %get-tuple-element.5) | copy-start | bytes 1769476

commit v3 on v2

--- a/solution.py
+++ b/solution.py
@@ -9,7 +9,7 @@
 
 MESH = pl.DeviceIdType.MESH
 TEXT, IMAGE = 0, 1
-HALVES = 2
+CHUNKS = 4
 
 
 def kernel(
@@ -141,7 +141,7 @@
     outer, z = lax.axis_index("outer"), lax.axis_index("inner")
     above, below = lax.rem(outer + 1, m), lax.rem(outer + m - 1, m)
     rows = text.shape[0]
-    half = rows // HALVES
+    size = rows // CHUNKS
     is_end = (z == 0) | (z == 3)
     is_middle = (z == 1) | (z == 2)
     high = (z >= 2).astype(jnp.int32)
@@ -172,29 +172,39 @@
             device_id=(o, i), device_id_type=MESH,
         )
 
-    def along(src, slot, way, to):
-        return remote(src, group.at[slot], line_send.at[slot, way], line_recv.at[slot], outer, to)
+    def piece(c):
+        return pl.ds(c * size, size)
+
+    def along(src, slot, way, to, c):
+        return remote(
+            src.at[piece(c)], group.at[slot, piece(c)],
+            line_send.at[slot, way, c], line_recv.at[slot, c], outer, to,
+        )
 
     def across(src, slot):
         return remote(src, guest.at[slot], side_send.at[slot], side_recv.at[slot], above, z)
 
-    def image_inward():
-        return remote(image, images.at[1], image_send.at[0], image_recv.at[0], outer, middle)
-
-    def image_across(src, i):
-        return remote(src, guest_images.at[i], guest_send.at[i], guest_recv.at[i], below, z)
-
-    def part(i, h):
-        rows_h = pl.ds(h * half, half)
+    def image_inward(c):
         return remote(
-            part_out.at[i, rows_h], part_in.at[i, rows_h],
-            part_send.at[i, h], part_recv.at[i, h], outer, far_middle,
-        )
-
-    def row_block(h):
-        rows_h = pl.ds(h * half, half)
+            image.at[piece(c)], images.at[1, piece(c)],
+            image_send.at[c], image_recv.at[c], outer, middle,
+        )
+
+    def image_across(src, i, c):
         return remote(
-            row_out.at[rows_h], row_in.at[rows_h], row_send.at[h], row_recv.at[h], outer, end
+            src.at[piece(c)], guest_images.at[i, piece(c)],
+            guest_send.at[i, c], guest_recv.at[i, c], below, z,
+        )
+
+    def part(i, c):
+        return remote(
+            part_out.at[i, piece(c)], part_in.at[i, piece(c)],
+            part_send.at[i, c], part_recv.at[i, c], outer, far_middle,
+        )
+
+    def row_block(c):
+        return remote(
+            row_out.at[piece(c)], row_in.at[piece(c)], row_send.at[c], row_recv.at[c], outer, end
         )
 
     def pair(left, right, positive):
@@ -219,107 +229,131 @@
         term = pair(left[...], block, positive)
         total[i] = term if first else total[i] + term
 
-    def arrive(slot):
-        along(text, slot, 0, end).wait_recv()
-
     def visit(slot):
         across(text, slot).wait_recv()
         add_image(guest.at[slot])
 
+    chunks = range(CHUNKS)
+
     @pl.when(is_end)
     def _():
-        along(text, z, 0, middle).start()
-        image_inward().start()
+        for c in chunks:
+            along(text, z, 0, middle, c).start()
         across(text, z).start()
         for load in loads:
             load.wait()
+        for c in chunks[:-1]:
+            along(text, z, 0, middle, c).wait_send()
+        for c in chunks:
+            image_inward(c).start()
         add_image(mine, positive=True, first=True)
         visit(z)
         for slot, previous in ((middle, None), (far_middle, middle), (far_end, far_middle)):
-            arrive(slot)
+            for c in chunks:
+                along(text, slot, 0, end, c).wait_recv()
             across(group.at[slot], slot).start()
             add_image(group.at[slot])
             if previous is not None:
                 visit(previous)
         visit(far_end)
-        for h in range(HALVES):
-            row_block(h).wait_recv()
-            rows_h = pl.ds(h * half, half)
-            grad_text[rows_h, :] = row_in[rows_h, :].astype(jnp.float32)
-        along(text, z, 0, middle).wait_send()
-        image_inward().wait_send()
+        for c in chunks:
+            row_block(c).wait_recv()
+            grad_text[piece(c), :] = row_in[piece(c), :].astype(jnp.float32)
+        along(text, z, 0, middle, CHUNKS - 1).wait_send()
+        for c in chunks:
+            image_inward(c).wait_send()
 
     @pl.when(is_middle)
     def _():
-        along(text, z, 0, far_middle).start()
-        along(text, z, 1, end).start()
-        image_across(image, 0).start()
+        own, beside, over, far = mine, group.at[end], group.at[far_middle], group.at[far_end]
+        for c in chunks:
+            along(text, z, 0, far_middle, c).start()
+        for c in chunks:
+            along(text, z, 1, end, c).start()
+        for c in chunks:
+            image_across(image, 0, c).start()
         across(text, z).start()
         for load in loads:
             load.wait()
-        add_image(mine, positive=True, first=True)
-        add_text(0, mine, images.at[0], positive=True, first=True)
-        image_across(image, 0).wait_recv()
-        add_text(0, mine, guest_images.at[0])
-
-        arrive(end)
-        along(group.at[end], end, 0, far_middle).start()
-        across(group.at[end], end).start()
-        add_text(1, group.at[end], images.at[0], first=True)
-        arrive(far_middle)
-        along(group.at[far_middle], far_middle, 0, end).start()
-        across(group.at[far_middle], far_middle).start()
-        add_text(2, group.at[far_middle], images.at[0], first=True)
-        add_text(2, group.at[far_middle], guest_images.at[0])
-
-        image_inward().wait_recv()
-        image_across(images.at[1], 1).start()
-        arrive(far_end)
-        along(group.at[far_end], far_end, 0, end).start()
-        across(group.at[far_end], far_end).start()
-        add_text(3, group.at[far_end], images.at[0], first=True)
-        add_text(3, group.at[far_end], guest_images.at[0])
-        add_text(3, group.at[far_end], images.at[1])
-        add_text(2, group.at[far_middle], images.at[1])
-        image_across(image, 1).wait_recv()
-        for i, slot, to in ((3, far_end, 1), (2, far_middle, 0)):
-            add_text(i, group.at[slot], guest_images.at[1])
-            part_out[to] = total[i].astype(jnp.bfloat16)
-            for h in range(HALVES):
-                part(to, h).start()
-
-        add_text(1, group.at[end], guest_images.at[0])
-        add_text(1, group.at[end], images.at[1], positive=True)
-        add_text(1, group.at[end], guest_images.at[1])
-        for h in range(HALVES):
-            part(1, h).wait_recv()
-            rows_h = pl.ds(h * half, half)
-            row_out[rows_h, :] = (
-                total[1, rows_h, :] + part_in[1, rows_h, :].astype(jnp.float32)
+        add_image(own, positive=True, first=True)
+        for c in chunks:
+            along(text, end, 0, middle, c).wait_recv()
+            along(beside, end, 0, far_middle, c).start()
+        add_text(0, own, images.at[0], positive=True, first=True)
+        add_text(1, beside, images.at[0], first=True)
+        for c in chunks:
+            along(text, far_middle, 0, middle, c).wait_recv()
+            along(over, far_middle, 0, end, c).start()
+        across(beside, end).start()
+        add_text(2, over, images.at[0], first=True)
+        for c in chunks:
+            image_across(image, 0, c).wait_recv()
+        early = (
+            lambda: add_text(2, over, guest_images.at[0]),
+            lambda: add_text(1, beside, guest_images.at[0]),
+            lambda: add_text(0, own, guest_images.at[0]),
+            lambda: add_image(beside),
+        )
+        for c in chunks:
+            early[c]()
+            image_inward(c).wait_recv()
+            image_across(images.at[1], 1, c).start()
+            along(text, far_end, 0, middle, c).wait_recv()
+            along(far, far_end, 0, end, c).start()
+        across(over, far_middle).start()
+        add_text(3, far, images.at[0], first=True)
+        add_text(3, far, guest_images.at[0])
+        add_text(3, far, images.at[1])
+        add_text(2, over, images.at[1])
+        for c in chunks:
+            image_across(image, 1, c).wait_recv()
+        add_text(3, far, guest_images.at[1])
+        for c in chunks:
+            part_out[1, piece(c), :] = total[3, piece(c), :].astype(jnp.bfloat16)
+            part(1, c).start()
+        across(far, far_end).start()
+        add_text(2, over, guest_images.at[1])
+        part_out[0] = total[2].astype(jnp.bfloat16)
+        add_text(1, beside, images.at[1], positive=True)
+        add_text(1, beside, guest_images.at[1])
+        for c in chunks[:-1]:
+            part(1, c).wait_send()
+        for c in chunks:
+            part(0, c).start()
+        late = (
+            lambda: add_image(over),
+            lambda: add_image(far),
+            lambda: visit(z),
+            lambda: visit(end),
+        )
+        for c in chunks:
+            part(1, c).wait_recv()
+            row_out[piece(c), :] = (
+                total[1, piece(c), :] + part_in[1, piece(c), :].astype(jnp.float32)
             ).astype(jnp.bfloat16)
-            row_block(h).start()
-        add_text(0, mine, images.at[1])
-        add_text(0, mine, guest_images.at[1])
-        for slot in (end, far_middle, far_end):
-            add_image(group.at[slot])
-        for slot in (z, end, far_middle, far_end):
-            visit(slot)
-        for h in range(HALVES):
-            part(0, h).wait_recv()
-            rows_h = pl.ds(h * half, half)
-            grad_text[rows_h, :] = total[0, rows_h, :] + part_in[0, rows_h, :].astype(jnp.float32)
-
-        along(text, z, 0, far_middle).wait_send()
-        along(text, z, 1, end).wait_send()
-        along(text, end, 0, far_middle).wait_send()
-        along(text, far_middle, 0, end).wait_send()
-        along(text, far_end, 0, end).wait_send()
-        for i in (0, 1):
-            image_across(image, i).wait_send()
-            for h in range(HALVES):
-                part(i, h).wait_send()
-        for h in range(HALVES):
-            row_block(h).wait_send()
+            row_block(c).start()
+            late[c]()
+        add_text(0, own, images.at[1])
+        add_text(0, own, guest_images.at[1])
+        visit(far_middle)
+        visit(far_end)
+        for c in chunks:
+            part(0, c).wait_recv()
+            grad_text[piece(c), :] = (
+                total[0, piece(c), :] + part_in[0, piece(c), :].astype(jnp.float32)
+            )
+
+        part(1, CHUNKS - 1).wait_send()
+        for c in chunks:
+            along(text, z, 0, far_middle, c).wait_send()
+            along(text, z, 1, end, c).wait_send()
+            along(text, end, 0, far_middle, c).wait_send()
+            along(text, far_middle, 0, end, c).wait_send()
+            along(text, far_end, 0, end, c).wait_send()
+            image_across(image, 0, c).wait_send()
+            image_across(image, 1, c).wait_send()
+            part(0, c).wait_send()
+            row_block(c).wait_send()
 
     for slot in range(4):
         across(text, slot).wait_send()
@@ -345,9 +379,9 @@
                 pltpu.VMEM((2, *block), jnp.bfloat16),
                 pltpu.VMEM(block, jnp.bfloat16),
                 pltpu.VMEM(block, jnp.bfloat16),
-                dma((2,)), dma((4, 2)), dma((4,)), dma((4,)), dma((4,)),
-                dma((1,)), dma((1,)), dma((2,)), dma((2,)),
-                dma((2, HALVES)), dma((2, HALVES)), dma((HALVES,)), dma((HALVES,)),
+                dma((2,)), dma((4, 2, CHUNKS)), dma((4, CHUNKS)), dma((4,)), dma((4,)),
+                dma((CHUNKS,)), dma((CHUNKS,)), dma((2, CHUNKS)), dma((2, CHUNKS)),
+                dma((2, CHUNKS)), dma((2, CHUNKS)), dma((CHUNKS,)), dma((CHUNKS,)),
             ]
         else:
             body = functools.partial(kernel, n, m)
@@ -359,13 +393,13 @@
             ]
         return pl.pallas_call(
             body,
-            out_shape=(jax.ShapeDtypeStruct((rows, width), jnp.float32),) * 2,
-            in_specs=[pl.BlockSpec(memory_space=pl.ANY)] * 2
+            out_shape=(pltpu.VMEM((rows, width), jnp.float32),) * 2,
+            in_specs=[pl.BlockSpec(memory_space=pltpu.HBM)] * 2
             + [pl.BlockSpec(memory_space=pltpu.SMEM)] * 2,
             out_specs=(pl.BlockSpec(memory_space=pltpu.VMEM),) * 2,
             scratch_shapes=scratch,
             compiler_params=pltpu.CompilerParams(
-                collective_id=0, has_side_effects=True, vmem_limit_bytes=60 * 1024 * 1024
+                collective_id=0, has_side_effects=True, vmem_limit_bytes=32 * 1024 * 1024
             ),
             cost_estimate=pl.CostEstimate(
                 flops=16 * n * rows * rows * width,

time: 44.1 us -> 41.2 us (0.934)
  the two profiles are of different devices: /device:TPU:1 before, /device:TPU:9 now
where the time goes in v3:
time: 41.2 us; the launch traced here: 41 us
  Pallas kernels  35.5 us (86%)
  local copies, waits for them, and re-layouts  3.55 us (9%)
  between operations  1.94 us (5%)
    pallas_call x1, Pallas kernels, per_device(): pl.pallas_call(body, out_shape=(pltpu.VMEM((rows, width), jnp.float32),)...  35.5 us
    unnamed x6, local copies, waits for them, and re-layouts  3.55 us

profile of v3, /device:TPU:9, one launch (start us, length us, event | category | flops | bytes accessed | tf_op | source)
XLA Modules:
  0.0 41.0 jit_solution(3690650718112689439)
XLA Ops:
  1.9 0.0 copy-start
  1.9 1.0 %copy-done = bf16[128,1152]{1,0:T(8,128)(2,1)S(1)} copy-done((bf16[128,1152]{1,0:T(8,128)(2,1)S(1)}, bf16[128,1152]{1,0:T(8,128)(2,1)}, u32[]{:S(2)}) %copy-start) | copy-done | bytes 294936
  2.9 0.0 copy-start.1
  2.9 1.0 %copy-done.1 = bf16[128,1152]{1,0:T(8,128)(2,1)S(1)} copy-done((bf16[128,1152]{1,0:T(8,128)(2,1)S(1)}, bf16[128,1152]{1,0:T(8,128)(2,1)}, u32[]{:S(2)}) %copy-start.1) | copy-done | bytes 294936
  3.8 35.5 %shard_map.59 = (f32[128,1152]{1,0:T(8,128)S(1)}, f32[128,1152]{1,0:T(8,128)S(1)}) custom-call(bf16[128,1152]{1,0:T(8,128)(2,1)S(1)} %copy-done, bf16[128,1152]{1,0:T(8,128)(2,1)S(1)} %copy-done.1, f32[1]{0:T(128)S(6)} %copy.10.scale, f32[1]{0:T(128)S(6)} %copy.11.offset), custom_call_target="tpu_custom_call" | custom-call | flops 1207959552 | bytes 1769472 | tf_op jit(solution)/shard_map/pallas_call | solution.py:394
  39.4 0.8 %copy.8 = f32[128,1152]{1,0:T(8,128)} copy(f32[128,1152]{1,0:T(8,128)S(1)} %get-tuple-element.2) | data formatting | bytes 1179648
  40.2 0.8 %copy.9 = f32[128,1152]{1,0:T(8,128)} copy(f32[128,1152]{1,0:T(8,128)S(1)} %get-tuple-element.3) | data formatting | bytes 1179648
Async XLA Ops:
  1.9 1.0 %copy-start = (bf16[128,1152]{1,0:T(8,128)(2,1)S(1)}, bf16[128,1152]{1,0:T(8,128)(2,1)}, u32[]{:S(2)}) copy-start(bf16[128,1152]{1,0:T(8,128)(2,1)} %image.1) | copy-start | bytes 884740
  2.9 1.0 %copy-start.1 = (bf16[128,1152]{1,0:T(8,128)(2,1)S(1)}, bf16[128,1152]{1,0:T(8,128)(2,1)}, u32[]{:S(2)}) copy-start(bf16[128,1152]{1,0:T(8,128)(2,1)} %text.1) | copy-start | bytes 884740

commit v4 on v3

--- a/solution.py
+++ b/solution.py
@@ -134,13 +134,13 @@
 
 def line4_kernel(
     m, image, text, scale, offset, grad_image, grad_text,
-    mine, group, guest, images, guest_images, total, part_out, part_in, row_out, row_in,
+    group, guest, images, total, part_out, part_in, row_out, row_in,
     load_sem, line_send, line_recv, side_send, side_recv, image_send, image_recv,
-    guest_send, guest_recv, part_send, part_recv, row_send, row_recv,
+    guest_send, guest_recv, part_send, part_recv, row_send, row_recv, turn,
 ):
     outer, z = lax.axis_index("outer"), lax.axis_index("inner")
     above, below = lax.rem(outer + 1, m), lax.rem(outer + m - 1, m)
-    rows = text.shape[0]
+    rows, width = text.shape
     size = rows // CHUNKS
     is_end = (z == 0) | (z == 3)
     is_middle = (z == 1) | (z == 2)
@@ -150,7 +150,7 @@
 
     loads = [
         pltpu.make_async_copy(image, images.at[0], load_sem.at[0]),
-        pltpu.make_async_copy(text, mine, load_sem.at[1]),
+        pltpu.make_async_copy(text, group.at[z], load_sem.at[1]),
     ]
     for load in loads:
         load.start()
@@ -192,7 +192,7 @@
 
     def image_across(src, i, c):
         return remote(
-            src.at[piece(c)], guest_images.at[i, piece(c)],
+            src.at[piece(c)], images.at[2 + i, piece(c)],
             guest_send.at[i, c], guest_recv.at[i, c], below, z,
         )
 
@@ -207,31 +207,28 @@
             row_out.at[piece(c)], row_in.at[piece(c)], row_send.at[c], row_recv.at[c], outer, end
         )
 
-    def pair(left, right, positive):
+    def pair(left, blocks, match=None):
+        right = blocks[...].reshape(-1, width)
         product = lax.dot_general(
-            left, right[...], (((1,), (1,)), ((), ())), preferred_element_type=jnp.float32
+            left, right, (((1,), (1,)), ((), ())), preferred_element_type=jnp.float32
         )
         logit = scale[0] * product + offset[0]
-        if positive:
-            row = lax.broadcasted_iota(jnp.int32, (rows, rows), 0)
-            column = lax.broadcasted_iota(jnp.int32, (rows, rows), 1)
-            sign = jnp.where(row == column, 1.0, -1.0)
+        if match is not None:
+            row = lax.broadcasted_iota(jnp.int32, logit.shape, 0)
+            column = lax.broadcasted_iota(jnp.int32, logit.shape, 1)
+            sign = jnp.where(column == row + match, 1.0, -1.0)
             coef = -sign * jax.nn.sigmoid(-sign * logit) * scale[0]
         else:
             coef = jax.nn.sigmoid(logit) * scale[0]
-        return jnp.dot(coef.astype(jnp.bfloat16), right[...], preferred_element_type=jnp.float32)
-
-    def add_image(block, positive=False, first=False):
-        term = pair(images[0], block, positive)
-        grad_image[...] = term if first else grad_image[...] + term
-
-    def add_text(i, left, block, positive=False, first=False):
-        term = pair(left[...], block, positive)
-        total[i] = term if first else total[i] + term
-
-    def visit(slot):
-        across(text, slot).wait_recv()
-        add_image(guest.at[slot])
+        return jnp.dot(coef.astype(jnp.bfloat16), right, preferred_element_type=jnp.float32)
+
+    def add_group():
+        grad_image[...] = pair(images[0], group, z * rows)
+
+    def add_guest():
+        for slot in range(4):
+            across(text, slot).wait_recv()
+        grad_image[...] += pair(images[0], guest)
 
     chunks = range(CHUNKS)
 
@@ -240,103 +237,81 @@
         for c in chunks:
             along(text, z, 0, middle, c).start()
         across(text, z).start()
+        for c in chunks[:-1]:
+            along(text, z, 0, middle, c).wait_send()
+        odd = lax.rem(outer, 2) == 1
+        pl.when(odd)(lambda: pl.semaphore_wait(turn, 1))
+        for c in chunks:
+            image_inward(c).start()
+        for c in chunks[:-1]:
+            image_inward(c).wait_send()
+        pl.when(jnp.logical_not(odd) & (outer + 1 < m))(
+            lambda: pl.semaphore_signal(
+                turn, inc=1, device_id=(above, z), device_id_type=MESH
+            )
+        )
         for load in loads:
             load.wait()
-        for c in chunks[:-1]:
-            along(text, z, 0, middle, c).wait_send()
-        for c in chunks:
-            image_inward(c).start()
-        add_image(mine, positive=True, first=True)
-        visit(z)
-        for slot, previous in ((middle, None), (far_middle, middle), (far_end, far_middle)):
+        for slot in (middle, far_middle, far_end):
             for c in chunks:
                 along(text, slot, 0, end, c).wait_recv()
             across(group.at[slot], slot).start()
-            add_image(group.at[slot])
-            if previous is not None:
-                visit(previous)
-        visit(far_end)
+        add_group()
+        add_guest()
         for c in chunks:
             row_block(c).wait_recv()
             grad_text[piece(c), :] = row_in[piece(c), :].astype(jnp.float32)
         along(text, z, 0, middle, CHUNKS - 1).wait_send()
-        for c in chunks:
-            image_inward(c).wait_send()
+        image_inward(CHUNKS - 1).wait_send()
 
     @pl.when(is_middle)
     def _():
-        own, beside, over, far = mine, group.at[end], group.at[far_middle], group.at[far_end]
+        beside, over, far = group.at[end], group.at[far_middle], group.at[far_end]
         for c in chunks:
             along(text, z, 0, far_middle, c).start()
-        for c in chunks:
             along(text, z, 1, end, c).start()
         for c in chunks:
             image_across(image, 0, c).start()
         across(text, z).start()
         for load in loads:
             load.wait()
-        add_image(own, positive=True, first=True)
         for c in chunks:
             along(text, end, 0, middle, c).wait_recv()
             along(beside, end, 0, far_middle, c).start()
-        add_text(0, own, images.at[0], positive=True, first=True)
-        add_text(1, beside, images.at[0], first=True)
+        across(beside, end).start()
         for c in chunks:
             along(text, far_middle, 0, middle, c).wait_recv()
             along(over, far_middle, 0, end, c).start()
-        across(beside, end).start()
-        add_text(2, over, images.at[0], first=True)
-        for c in chunks:
-            image_across(image, 0, c).wait_recv()
-        early = (
-            lambda: add_text(2, over, guest_images.at[0]),
-            lambda: add_text(1, beside, guest_images.at[0]),
-            lambda: add_text(0, own, guest_images.at[0]),
-            lambda: add_image(beside),
-        )
-        for c in chunks:
-            early[c]()
+        across(over, far_middle).start()
+        for c in chunks:
             image_inward(c).wait_recv()
             image_across(images.at[1], 1, c).start()
+        for c in chunks:
             along(text, far_end, 0, middle, c).wait_recv()
             along(far, far_end, 0, end, c).start()
-        across(over, far_middle).start()
-        add_text(3, far, images.at[0], first=True)
-        add_text(3, far, guest_images.at[0])
-        add_text(3, far, images.at[1])
-        add_text(2, over, images.at[1])
-        for c in chunks:
+        for c in chunks:
+            image_across(image, 0, c).wait_recv()
             image_across(image, 1, c).wait_recv()
-        add_text(3, far, guest_images.at[1])
-        for c in chunks:
-            part_out[1, piece(c), :] = total[3, piece(c), :].astype(jnp.bfloat16)
+        part_out[1] = pair(far[...], images).astype(jnp.bfloat16)
+        for c in chunks:
             part(1, c).start()
         across(far, far_end).start()
-        add_text(2, over, guest_images.at[1])
-        part_out[0] = total[2].astype(jnp.bfloat16)
-        add_text(1, beside, images.at[1], positive=True)
-        add_text(1, beside, guest_images.at[1])
-        for c in chunks[:-1]:
-            part(1, c).wait_send()
-        for c in chunks:
-            part(0, c).start()
-        late = (
-            lambda: add_image(over),
-            lambda: add_image(far),
-            lambda: visit(z),
-            lambda: visit(end),
-        )
+        part_out[0] = pair(over[...], images).astype(jnp.bfloat16)
+        total[1] = pair(beside[...], images, rows)
+        add_group()
         for c in chunks:
             part(1, c).wait_recv()
             row_out[piece(c), :] = (
                 total[1, piece(c), :] + part_in[1, piece(c), :].astype(jnp.float32)
             ).astype(jnp.bfloat16)
             row_block(c).start()
-            late[c]()
-        add_text(0, own, images.at[1])
-        add_text(0, own, guest_images.at[1])
-        visit(far_middle)
-        visit(far_end)
+            if c == CHUNKS - 2:
+                for early in chunks[:-1]:
+                    part(1, early).wait_send()
+                for late in chunks:
+                    part(0, late).start()
+        total[0] = pair(group[z], images, 0)
+        add_guest()
         for c in chunks:
             part(0, c).wait_recv()
             grad_text[piece(c), :] = (
@@ -369,12 +344,10 @@
         if n == 4:
             body = functools.partial(line4_kernel, m)
             scratch = [
-                pltpu.VMEM(block, jnp.bfloat16),
                 pltpu.VMEM((4, *block), jnp.bfloat16),
                 pltpu.VMEM((4, *block), jnp.bfloat16),
-                pltpu.VMEM((2, *block), jnp.bfloat16),
-                pltpu.VMEM((2, *block), jnp.bfloat16),
-                pltpu.VMEM((4, *block), jnp.float32),
+                pltpu.VMEM((4, *block), jnp.bfloat16),
+                pltpu.VMEM((2, *block), jnp.float32),
                 pltpu.VMEM((2, *block), jnp.bfloat16),
                 pltpu.VMEM((2, *block), jnp.bfloat16),
                 pltpu.VMEM(block, jnp.bfloat16),
@@ -382,6 +355,7 @@
                 dma((2,)), dma((4, 2, CHUNKS)), dma((4, CHUNKS)), dma((4,)), dma((4,)),
                 dma((CHUNKS,)), dma((CHUNKS,)), dma((2, CHUNKS)), dma((2, CHUNKS)),
                 dma((2, CHUNKS)), dma((2, CHUNKS)), dma((CHUNKS,)), dma((CHUNKS,)),
+                pltpu.SemaphoreType.REGULAR,
             ]
         else:
             body = functools.partial(kernel, n, m)
@@ -399,7 +373,7 @@
             out_specs=(pl.BlockSpec(memory_space=pltpu.VMEM),) * 2,
             scratch_shapes=scratch,
             compiler_params=pltpu.CompilerParams(
-                collective_id=0, has_side_effects=True, vmem_limit_bytes=32 * 1024 * 1024
+                collective_id=0, has_side_effects=True, vmem_limit_bytes=58 * 1024 * 1024
             ),
             cost_estimate=pl.CostEstimate(
                 flops=16 * n * rows * rows * width,

time: 41.2 us -> 40.2 us (0.976)
  local copies, waits for them, and re-layouts: 3.55 us -> 1.63 us
  Pallas kernels: 35.5 us -> 36.4 us
    unnamed x6 -> x2, local copies, waits for them, and re-layouts: 3.55 us -> 1.63 us
    pallas_call x1, Pallas kernels: 35.5 us -> 36.4 us  [per_device(): pl.pallas_call(body, out_shape=(pltpu.VMEM((rows, width), jnp.float32),)...]
where the time goes in v4:
time: 40.2 us; the launch traced here: 40 us
  Pallas kernels  36.4 us (91%)
  between operations  1.93 us (5%)
  local copies, waits for them, and re-layouts  1.63 us (4%)
    pallas_call x1, Pallas kernels, per_device(): pl.pallas_call(body, out_shape=(pltpu.VMEM((rows, width), jnp.float32),)...  36.4 us
    unnamed x2, local copies, waits for them, and re-layouts  1.63 us

profile of v4, /device:TPU:9, one launch (start us, length us, event | category | flops | bytes accessed | tf_op | source)
XLA Modules:
  0.0 40.0 jit_solution(14375645334060879238)
XLA Ops:
  1.9 36.4 %shard_map.59 = (f32[128,1152]{1,0:T(8,128)S(1)}, f32[128,1152]{1,0:T(8,128)S(1)}) custom-call(bf16[128,1152]{1,0:T(8,128)(2,1)} %image.1, bf16[128,1152]{1,0:T(8,128)(2,1)} %text.1, f32[1]{0:T(128)S(6)} %copy.10.scale, f32[1]{0:T(128)S(6)} %copy.11.offset), custom_call_target="tpu_custom_call" | custom-call | flops 1207959552 | bytes 1769472 | tf_op jit(solution)/shard_map/pallas_call | solution.py:368
  38.4 0.8 %copy.8 = f32[128,1152]{1,0:T(8,128)} copy(f32[128,1152]{1,0:T(8,128)S(1)} %get-tuple-element.2) | data formatting | bytes 1179648
  39.2 0.8 %copy.9 = f32[128,1152]{1,0:T(8,128)} copy(f32[128,1152]{1,0:T(8,128)S(1)} %get-tuple-element.3) | data formatting | bytes 1179648

commit v5 on v4

--- a/solution.py
+++ b/solution.py
@@ -10,6 +10,7 @@
 MESH = pl.DeviceIdType.MESH
 TEXT, IMAGE = 0, 1
 CHUNKS = 4
+BANDS = 3
 
 
 def kernel(
@@ -141,7 +142,7 @@
     outer, z = lax.axis_index("outer"), lax.axis_index("inner")
     above, below = lax.rem(outer + 1, m), lax.rem(outer + m - 1, m)
     rows, width = text.shape
-    size = rows // CHUNKS
+    size, band = rows // CHUNKS, width // BANDS
     is_end = (z == 0) | (z == 3)
     is_middle = (z == 1) | (z == 2)
     high = (z >= 2).astype(jnp.int32)
@@ -186,29 +187,32 @@
 
     def image_inward(c):
         return remote(
-            image.at[piece(c)], images.at[1, piece(c)],
+            image.at[piece(c)], images.at[2, piece(c)],
             image_send.at[c], image_recv.at[c], outer, middle,
         )
 
     def image_across(src, i, c):
         return remote(
-            src.at[piece(c)], images.at[2 + i, piece(c)],
+            src.at[piece(c)], images.at[1 + 2 * i, piece(c)],
             guest_send.at[i, c], guest_recv.at[i, c], below, z,
         )
+
+    def columns(c):
+        return pl.ds(c * band, band)
 
     def part(i, c):
         return remote(
-            part_out.at[i, piece(c)], part_in.at[i, piece(c)],
+            part_out.at[i, :, columns(c)], part_in.at[i, :, columns(c)],
             part_send.at[i, c], part_recv.at[i, c], outer, far_middle,
         )
 
     def row_block(c):
         return remote(
-            row_out.at[piece(c)], row_in.at[piece(c)], row_send.at[c], row_recv.at[c], outer, end
-        )
-
-    def pair(left, blocks, match=None):
-        right = blocks[...].reshape(-1, width)
+            row_out.at[:, columns(c)], row_in.at[:, columns(c)],
+            row_send.at[c], row_recv.at[c], outer, end,
+        )
+
+    def weigh(left, right, match=None):
         product = lax.dot_general(
             left, right, (((1,), (1,)), ((), ())), preferred_element_type=jnp.float32
         )
@@ -220,7 +224,12 @@
             coef = -sign * jax.nn.sigmoid(-sign * logit) * scale[0]
         else:
             coef = jax.nn.sigmoid(logit) * scale[0]
-        return jnp.dot(coef.astype(jnp.bfloat16), right, preferred_element_type=jnp.float32)
+        return coef.astype(jnp.bfloat16)
+
+    def pair(left, blocks, match=None):
+        right = blocks[...].reshape(-1, width)
+        coef = weigh(left, right, match)
+        return jnp.dot(coef, right, preferred_element_type=jnp.float32)
 
     def add_group():
         grad_image[...] = pair(images[0], group, z * rows)
@@ -230,7 +239,7 @@
             across(text, slot).wait_recv()
         grad_image[...] += pair(images[0], guest)
 
-    chunks = range(CHUNKS)
+    chunks, bands = range(CHUNKS), range(BANDS)
 
     @pl.when(is_end)
     def _():
@@ -258,9 +267,9 @@
             across(group.at[slot], slot).start()
         add_group()
         add_guest()
-        for c in chunks:
+        for c in bands:
             row_block(c).wait_recv()
-            grad_text[piece(c), :] = row_in[piece(c), :].astype(jnp.float32)
+            grad_text[:, columns(c)] = row_in[:, columns(c)].astype(jnp.float32)
         along(text, z, 0, middle, CHUNKS - 1).wait_send()
         image_inward(CHUNKS - 1).wait_send()
 
@@ -283,42 +292,53 @@
             along(text, far_middle, 0, middle, c).wait_recv()
             along(over, far_middle, 0, end, c).start()
         across(over, far_middle).start()
-        for c in chunks:
+        first, second = images.at[pl.ds(0, 2)], images.at[pl.ds(2, 2)]
+        for c in chunks:
+            image_across(image, 0, c).wait_recv()
+        total[2] = pair(over[...], first)
+        total[1] = pair(beside[...], first)
+        for c in chunks:
+            if c == CHUNKS // 2:
+                total[0] = pair(group[z], first, 0)
             image_inward(c).wait_recv()
-            image_across(images.at[1], 1, c).start()
+            image_across(images.at[2], 1, c).start()
         for c in chunks:
             along(text, far_end, 0, middle, c).wait_recv()
             along(far, far_end, 0, end, c).start()
         for c in chunks:
-            image_across(image, 0, c).wait_recv()
             image_across(image, 1, c).wait_recv()
-        part_out[1] = pair(far[...], images).astype(jnp.bfloat16)
-        for c in chunks:
+        coef = weigh(far[...], images[...].reshape(-1, width))
+        for c in bands:
+            part_out[1, :, columns(c)] = jnp.dot(
+                coef,
+                images[:, :, columns(c)].reshape(-1, band),
+                preferred_element_type=jnp.float32,
+            ).astype(jnp.bfloat16)
             part(1, c).start()
         across(far, far_end).start()
-        part_out[0] = pair(over[...], images).astype(jnp.bfloat16)
-        total[1] = pair(beside[...], images, rows)
-        add_group()
-        for c in chunks:
+        part_out[0] = (total[2] + pair(over[...], second)).astype(jnp.bfloat16)
+        total[1] += pair(beside[...], second, 0)
+        for c in bands:
             part(1, c).wait_recv()
-            row_out[piece(c), :] = (
-                total[1, piece(c), :] + part_in[1, piece(c), :].astype(jnp.float32)
+            row_out[:, columns(c)] = (
+                total[1, :, columns(c)] + part_in[1, :, columns(c)].astype(jnp.float32)
             ).astype(jnp.bfloat16)
             row_block(c).start()
-            if c == CHUNKS - 2:
-                for early in chunks[:-1]:
+            if c == BANDS - 2:
+                for early in bands[:-1]:
                     part(1, early).wait_send()
-                for late in chunks:
+                for late in bands:
                     part(0, late).start()
-        total[0] = pair(group[z], images, 0)
+        total[0] += pair(group[z], second)
+        add_group()
         add_guest()
-        for c in chunks:
+        for c in bands:
             part(0, c).wait_recv()
-            grad_text[piece(c), :] = (
-                total[0, piece(c), :] + part_in[0, piece(c), :].astype(jnp.float32)
+            grad_text[:, columns(c)] = (
+                total[0, :, columns(c)] + part_in[0, :, columns(c)].astype(jnp.float32)
             )
 
-        part(1, CHUNKS - 1).wait_send()
+        part(1, BANDS - 1).wait_send()
         for c in chunks:
             along(text, z, 0, far_middle, c).wait_send()
             along(text, z, 1, end, c).wait_send()
@@ -327,11 +347,27 @@
             along(text, far_end, 0, end, c).wait_send()
             image_across(image, 0, c).wait_send()
             image_across(image, 1, c).wait_send()
+        for c in bands:
             part(0, c).wait_send()
             row_block(c).wait_send()
 
     for slot in range(4):
         across(text, slot).wait_send()
+
+
+def store_kernel(image_in, text_in, image_out, text_out, sem):
+    size = image_in.shape[0] // CHUNKS
+    copies = [
+        pltpu.make_async_copy(
+            src.at[pl.ds(c * size, size)], dst.at[pl.ds(c * size, size)], sem.at[k, c]
+        )
+        for k, (src, dst) in enumerate(((image_in, image_out), (text_in, text_out)))
+        for c in range(CHUNKS)
+    ]
+    for copy in copies:
+        copy.start()
+    for copy in copies:
+        copy.wait()
 
 
 def solution(mesh):
@@ -347,14 +383,14 @@
                 pltpu.VMEM((4, *block), jnp.bfloat16),
                 pltpu.VMEM((4, *block), jnp.bfloat16),
                 pltpu.VMEM((4, *block), jnp.bfloat16),
-                pltpu.VMEM((2, *block), jnp.float32),
+                pltpu.VMEM((3, *block), jnp.float32),
                 pltpu.VMEM((2, *block), jnp.bfloat16),
                 pltpu.VMEM((2, *block), jnp.bfloat16),
                 pltpu.VMEM(block, jnp.bfloat16),
                 pltpu.VMEM(block, jnp.bfloat16),
                 dma((2,)), dma((4, 2, CHUNKS)), dma((4, CHUNKS)), dma((4,)), dma((4,)),
                 dma((CHUNKS,)), dma((CHUNKS,)), dma((2, CHUNKS)), dma((2, CHUNKS)),
-                dma((2, CHUNKS)), dma((2, CHUNKS)), dma((CHUNKS,)), dma((CHUNKS,)),
+                dma((2, BANDS)), dma((2, BANDS)), dma((BANDS,)), dma((BANDS,)),
                 pltpu.SemaphoreType.REGULAR,
             ]
         else:
@@ -365,7 +401,7 @@
                 pltpu.VMEM((2, n, *block), jnp.bfloat16),
                 dma((2,)), dma((2, n, 2)), dma((2, n)), dma((2, n)), dma((2, n)),
             ]
-        return pl.pallas_call(
+        grads = pl.pallas_call(
             body,
             out_shape=(pltpu.VMEM((rows, width), jnp.float32),) * 2,
             in_specs=[pl.BlockSpec(memory_space=pltpu.HBM)] * 2
@@ -381,6 +417,13 @@
                 transcendentals=4 * n * rows * rows,
             ),
         )(image, text, scale, offset)
+        return pl.pallas_call(
+            store_kernel,
+            out_shape=(jax.ShapeDtypeStruct(block, jnp.float32),) * 2,
+            in_specs=[pl.BlockSpec(memory_space=pl.ANY)] * 2,
+            out_specs=(pl.BlockSpec(memory_space=pl.ANY),) * 2,
+            scratch_shapes=[dma((2, CHUNKS))],
+        )(*grads)
 
     return jax.shard_map(
         per_device,

time: 40.2 us -> 76.9 us (1.91)
  the two profiles are of different devices: /device:TPU:9 before, /device:TPU:0 now
where the time goes in v5:
time: 76.9 us; the launch traced here: 75.5 us
  Pallas kernels  71.9 us (93%)
  between operations  1.94 us (3%)
  local copies, waits for them, and re-layouts  1.61 us (2%)
    pallas_call x1, Pallas kernels, per_device(): pl.pallas_call(store_kernel, out_shape=(jax.ShapeDtypeStruct(block, jnp.f...  36.9 us
    pallas_call x1, Pallas kernels, per_device(): pl.pallas_call(body, out_shape=(pltpu.VMEM((rows, width), jnp.float32),)...  35 us
    unnamed x4, local copies, waits for them, and re-layouts  1.61 us

profile of v5, /device:TPU:0, one launch (start us, length us, event | category | flops | bytes accessed | tf_op | source)
XLA Modules:
  0.0 75.5 jit_solution(10062076022415627362)
XLA Ops:
  1.9 35.0 %shard_map.59 = (f32[128,1152]{1,0:T(8,128)S(1)}, f32[128,1152]{1,0:T(8,128)S(1)}) custom-call(bf16[128,1152]{1,0:T(8,128)(2,1)} %image.1, bf16[128,1152]{1,0:T(8,128)(2,1)} %text.1, f32[1]{0:T(128)S(6)} %copy.6.scale, f32[1]{0:T(128)S(6)} %copy.7.offset), custom_call_target="tpu_custom_call" | custom-call | flops 1207959552 | bytes 1769472 | tf_op jit(solution)/shard_map/pallas_call | solution.py:404
  37.0 0.0 copy-start
  37.0 0.8 %copy-done = f32[128,1152]{1,0:T(8,128)} copy-done((f32[128,1152]{1,0:T(8,128)}, f32[128,1152]{1,0:T(8,128)S(1)}, u32[]{:S(2)}) %copy-start) | copy-done | bytes 589848
  37.8 0.0 copy-start.1
  37.8 0.8 %copy-done.1 = f32[128,1152]{1,0:T(8,128)} copy-done((f32[128,1152]{1,0:T(8,128)}, f32[128,1152]{1,0:T(8,128)S(1)}, u32[]{:S(2)}) %copy-start.1) | copy-done | bytes 589848
  38.6 36.9 %shard_map.60 = (f32[128,1152]{1,0:T(8,128)}, f32[128,1152]{1,0:T(8,128)}) custom-call(f32[128,1152]{1,0:T(8,128)} %copy-done, f32[128,1152]{1,0:T(8,128)} %copy-done.1), custom_call_target="tpu_custom_call" | custom-call | tf_op jit(solution)/shard_map/pallas_call | solution.py:420
Async XLA Ops:
  37.0 0.8 %copy-start = (f32[128,1152]{1,0:T(8,128)}, f32[128,1152]{1,0:T(8,128)S(1)}, u32[]{:S(2)}) copy-start(f32[128,1152]{1,0:T(8,128)S(1)} %get-tuple-element.4.image_in) | copy-start | bytes 1769476
  37.8 0.8 %copy-start.1 = (f32[128,1152]{1,0:T(8,128)}, f32[128,1152]{1,0:T(8,128)S(1)}, u32[]{:S(2)}) copy-start(f32[128,1152]{1,0:T(8,128)S(1)} %get-tuple-element.5.text_in) | copy-start | bytes 1769476

commit v6 on v4

--- a/solution.py
+++ b/solution.py
@@ -136,7 +136,7 @@
     m, image, text, scale, offset, grad_image, grad_text,
     group, guest, images, total, part_out, part_in, row_out, row_in,
     load_sem, line_send, line_recv, side_send, side_recv, image_send, image_recv,
-    guest_send, guest_recv, part_send, part_recv, row_send, row_recv, turn,
+    guest_send, guest_recv, part_send, part_recv, row_send, row_recv,
 ):
     outer, z = lax.axis_index("outer"), lax.axis_index("inner")
     above, below = lax.rem(outer + 1, m), lax.rem(outer + m - 1, m)
@@ -186,13 +186,13 @@
 
     def image_inward(c):
         return remote(
-            image.at[piece(c)], images.at[1, piece(c)],
+            image.at[piece(c)], images.at[2, piece(c)],
             image_send.at[c], image_recv.at[c], outer, middle,
         )
 
     def image_across(src, i, c):
         return remote(
-            src.at[piece(c)], images.at[2 + i, piece(c)],
+            src.at[piece(c)], images.at[1 + 2 * i, piece(c)],
             guest_send.at[i, c], guest_recv.at[i, c], below, z,
         )
 
@@ -207,8 +207,7 @@
             row_out.at[piece(c)], row_in.at[piece(c)], row_send.at[c], row_recv.at[c], outer, end
         )
 
-    def pair(left, blocks, match=None):
-        right = blocks[...].reshape(-1, width)
+    def weigh(left, right, match=None):
         product = lax.dot_general(
             left, right, (((1,), (1,)), ((), ())), preferred_element_type=jnp.float32
         )
@@ -220,7 +219,12 @@
             coef = -sign * jax.nn.sigmoid(-sign * logit) * scale[0]
         else:
             coef = jax.nn.sigmoid(logit) * scale[0]
-        return jnp.dot(coef.astype(jnp.bfloat16), right, preferred_element_type=jnp.float32)
+        return coef.astype(jnp.bfloat16)
+
+    def pair(left, blocks, match=None):
+        right = blocks[...].reshape(-1, width)
+        coef = weigh(left, right, match)
+        return jnp.dot(coef, right, preferred_element_type=jnp.float32)
 
     def add_group():
         grad_image[...] = pair(images[0], group, z * rows)
@@ -235,23 +239,14 @@
     @pl.when(is_end)
     def _():
         for c in chunks:
-            along(text, z, 0, middle, c).start()
+            image_inward(c).start()
         across(text, z).start()
-        for c in chunks[:-1]:
-            along(text, z, 0, middle, c).wait_send()
-        odd = lax.rem(outer, 2) == 1
-        pl.when(odd)(lambda: pl.semaphore_wait(turn, 1))
-        for c in chunks:
-            image_inward(c).start()
+        for load in loads:
+            load.wait()
         for c in chunks[:-1]:
             image_inward(c).wait_send()
-        pl.when(jnp.logical_not(odd) & (outer + 1 < m))(
-            lambda: pl.semaphore_signal(
-                turn, inc=1, device_id=(above, z), device_id_type=MESH
-            )
-        )
-        for load in loads:
-            load.wait()
+        for c in chunks:
+            along(text, z, 0, middle, c).start()
         for slot in (middle, far_middle, far_end):
             for c in chunks:
                 along(text, slot, 0, end, c).wait_recv()
@@ -261,12 +256,14 @@
         for c in chunks:
             row_block(c).wait_recv()
             grad_text[piece(c), :] = row_in[piece(c), :].astype(jnp.float32)
-        along(text, z, 0, middle, CHUNKS - 1).wait_send()
         image_inward(CHUNKS - 1).wait_send()
+        for c in chunks:
+            along(text, z, 0, middle, c).wait_send()
 
     @pl.when(is_middle)
     def _():
         beside, over, far = group.at[end], group.at[far_middle], group.at[far_end]
+        first, second = images.at[pl.ds(0, 2)], images.at[pl.ds(2, 2)]
         for c in chunks:
             along(text, z, 0, far_middle, c).start()
             along(text, z, 1, end, c).start()
@@ -276,29 +273,32 @@
         for load in loads:
             load.wait()
         for c in chunks:
-            along(text, end, 0, middle, c).wait_recv()
-            along(beside, end, 0, far_middle, c).start()
-        across(beside, end).start()
-        for c in chunks:
+            image_inward(c).wait_recv()
+            image_across(images.at[2], 1, c).start()
             along(text, far_middle, 0, middle, c).wait_recv()
             along(over, far_middle, 0, end, c).start()
         across(over, far_middle).start()
         for c in chunks:
-            image_inward(c).wait_recv()
-            image_across(images.at[1], 1, c).start()
+            image_across(image, 0, c).wait_recv()
+        total[2] = pair(over[...], first)
+        total[0] = pair(group[z], first, 0)
+        for c in chunks:
+            along(text, end, 0, middle, c).wait_recv()
+            along(beside, end, 0, far_middle, c).start()
+        for c in chunks:
+            image_across(image, 1, c).wait_recv()
+        part_out[0] = (total[2] + pair(over[...], second)).astype(jnp.bfloat16)
+        for c in chunks[: CHUNKS // 2]:
+            part(0, c).start()
+        across(beside, end).start()
         for c in chunks:
             along(text, far_end, 0, middle, c).wait_recv()
             along(far, far_end, 0, end, c).start()
-        for c in chunks:
-            image_across(image, 0, c).wait_recv()
-            image_across(image, 1, c).wait_recv()
         part_out[1] = pair(far[...], images).astype(jnp.bfloat16)
         for c in chunks:
             part(1, c).start()
         across(far, far_end).start()
-        part_out[0] = pair(over[...], images).astype(jnp.bfloat16)
-        total[1] = pair(beside[...], images, rows)
-        add_group()
+        total[1] = pair(beside[...], images, 2 * rows)
         for c in chunks:
             part(1, c).wait_recv()
             row_out[piece(c), :] = (
@@ -308,9 +308,10 @@
             if c == CHUNKS - 2:
                 for early in chunks[:-1]:
                     part(1, early).wait_send()
-                for late in chunks:
+                for late in chunks[CHUNKS // 2 :]:
                     part(0, late).start()
-        total[0] = pair(group[z], images, 0)
+        total[0] += pair(group[z], second)
+        add_group()
         add_guest()
         for c in chunks:
             part(0, c).wait_recv()
@@ -347,7 +348,7 @@
                 pltpu.VMEM((4, *block), jnp.bfloat16),
                 pltpu.VMEM((4, *block), jnp.bfloat16),
                 pltpu.VMEM((4, *block), jnp.bfloat16),
-                pltpu.VMEM((2, *block), jnp.float32),
+                pltpu.VMEM((3, *block), jnp.float32),
                 pltpu.VMEM((2, *block), jnp.bfloat16),
                 pltpu.VMEM((2, *block), jnp.bfloat16),
                 pltpu.VMEM(block, jnp.bfloat16),
@@ -355,7 +356,6 @@
                 dma((2,)), dma((4, 2, CHUNKS)), dma((4, CHUNKS)), dma((4,)), dma((4,)),
                 dma((CHUNKS,)), dma((CHUNKS,)), dma((2, CHUNKS)), dma((2, CHUNKS)),
                 dma((2, CHUNKS)), dma((2, CHUNKS)), dma((CHUNKS,)), dma((CHUNKS,)),
-                pltpu.SemaphoreType.REGULAR,
             ]
         else:
             body = functools.partial(kernel, n, m)

time: 40.2 us -> 41.9 us (1.042)
  the two profiles are of different devices: /device:TPU:9 before, /device:TPU:0 now
where the time goes in v6:
time: 41.9 us; the launch traced here: 41.8 us
  Pallas kernels  38.2 us (91%)
  between operations  1.93 us (5%)
  local copies, waits for them, and re-layouts  1.63 us (4%)
    pallas_call x1, Pallas kernels, per_device(): pl.pallas_call(body, out_shape=(pltpu.VMEM((rows, width), jnp.float32),)...  38.2 us
    unnamed x2, local copies, waits for them, and re-layouts  1.63 us

profile of v6, /device:TPU:0, one launch (start us, length us, event | category | flops | bytes accessed | tf_op | source)
XLA Modules:
  0.0 41.8 jit_solution(9577993007906364383)
XLA Ops:
  1.9 38.2 %shard_map.59 = (f32[128,1152]{1,0:T(8,128)S(1)}, f32[128,1152]{1,0:T(8,128)S(1)}) custom-call(bf16[128,1152]{1,0:T(8,128)(2,1)} %image.1, bf16[128,1152]{1,0:T(8,128)(2,1)} %text.1, f32[1]{0:T(128)S(6)} %copy.10.scale, f32[1]{0:T(128)S(6)} %copy.11.offset), custom_call_target="tpu_custom_call" | custom-call | flops 1207959552 | bytes 1769472 | tf_op jit(solution)/shard_map/pallas_call | solution.py:368
  40.1 0.8 %copy.8 = f32[128,1152]{1,0:T(8,128)} copy(f32[128,1152]{1,0:T(8,128)S(1)} %get-tuple-element.2) | data formatting | bytes 1179648
  40.9 0.8 %copy.9 = f32[128,1152]{1,0:T(8,128)} copy(f32[128,1152]{1,0:T(8,128)S(1)} %get-tuple-element.3) | data formatting | bytes 1179648

commit v7 on v6

--- a/solution.py
+++ b/solution.py
@@ -181,8 +181,11 @@
             line_send.at[slot, way, c], line_recv.at[slot, c], outer, to,
         )
 
-    def across(src, slot):
-        return remote(src, guest.at[slot], side_send.at[slot], side_recv.at[slot], above, z)
+    def across(src, slot, c):
+        return remote(
+            src.at[piece(c)], guest.at[slot, piece(c)],
+            side_send.at[slot, c], side_recv.at[slot, c], above, z,
+        )
 
     def image_inward(c):
         return remote(
@@ -226,13 +229,15 @@
         coef = weigh(left, right, match)
         return jnp.dot(coef, right, preferred_element_type=jnp.float32)
 
-    def add_group():
-        grad_image[...] = pair(images[0], group, z * rows)
-
-    def add_guest():
-        for slot in range(4):
-            across(text, slot).wait_recv()
-        grad_image[...] += pair(images[0], guest)
+    def add_group(slot, count, match=None, first=False):
+        term = pair(images[0], group.at[pl.ds(slot, count)], match)
+        grad_image[...] = term if first else grad_image[...] + term
+
+    def add_guest(slot, count):
+        for k in range(count):
+            for c in chunks:
+                across(text, slot + k, c).wait_recv()
+        grad_image[...] += pair(images[0], guest.at[pl.ds(slot, count)])
 
     chunks = range(CHUNKS)
 
@@ -240,19 +245,24 @@
     def _():
         for c in chunks:
             image_inward(c).start()
-        across(text, z).start()
+        for c in chunks:
+            across(text, z, c).start()
         for load in loads:
             load.wait()
         for c in chunks[:-1]:
             image_inward(c).wait_send()
         for c in chunks:
             along(text, z, 0, middle, c).start()
+        add_group(z, 1, 0, first=True)
         for slot in (middle, far_middle, far_end):
             for c in chunks:
                 along(text, slot, 0, end, c).wait_recv()
-            across(group.at[slot], slot).start()
-        add_group()
-        add_guest()
+                across(group.at[slot], slot, c).start()
+        add_group(1, 2)
+        add_group(far_end, 1)
+        add_guest(end, 1)
+        add_guest(1, 2)
+        add_guest(far_end, 1)
         for c in chunks:
             row_block(c).wait_recv()
             grad_text[piece(c), :] = row_in[piece(c), :].astype(jnp.float32)
@@ -269,7 +279,8 @@
             along(text, z, 1, end, c).start()
         for c in chunks:
             image_across(image, 0, c).start()
-        across(text, z).start()
+        for c in chunks:
+            across(text, z, c).start()
         for load in loads:
             load.wait()
         for c in chunks:
@@ -277,49 +288,61 @@
             image_across(images.at[2], 1, c).start()
             along(text, far_middle, 0, middle, c).wait_recv()
             along(over, far_middle, 0, end, c).start()
-        across(over, far_middle).start()
+            across(over, far_middle, c).start()
         for c in chunks:
             image_across(image, 0, c).wait_recv()
         total[2] = pair(over[...], first)
-        total[0] = pair(group[z], first, 0)
         for c in chunks:
             along(text, end, 0, middle, c).wait_recv()
             along(beside, end, 0, far_middle, c).start()
+            across(beside, end, c).start()
+            if c == 0:
+                total[0] = pair(group[z], first, 0)
+            if c == 1:
+                add_group(1, 2, (z - 1) * rows, first=True)
         for c in chunks:
             image_across(image, 1, c).wait_recv()
         part_out[0] = (total[2] + pair(over[...], second)).astype(jnp.bfloat16)
         for c in chunks[: CHUNKS // 2]:
             part(0, c).start()
-        across(beside, end).start()
         for c in chunks:
             along(text, far_end, 0, middle, c).wait_recv()
             along(far, far_end, 0, end, c).start()
+            across(far, far_end, c).start()
         part_out[1] = pair(far[...], images).astype(jnp.bfloat16)
         for c in chunks:
             part(1, c).start()
-        across(far, far_end).start()
         total[1] = pair(beside[...], images, 2 * rows)
+        total[0] += pair(group[z], second)
+        between = (
+            lambda: add_group(end, 1),
+            lambda: add_group(far_end, 1),
+            lambda: add_guest(1, 2),
+            lambda: add_guest(end, 1),
+        )
+        gate = CHUNKS // 2 - 1
         for c in chunks:
             part(1, c).wait_recv()
             row_out[piece(c), :] = (
                 total[1, piece(c), :] + part_in[1, piece(c), :].astype(jnp.float32)
             ).astype(jnp.bfloat16)
             row_block(c).start()
-            if c == CHUNKS - 2:
-                for early in chunks[:-1]:
+            if c == gate:
+                for early in chunks[: gate + 1]:
                     part(1, early).wait_send()
                 for late in chunks[CHUNKS // 2 :]:
                     part(0, late).start()
-        total[0] += pair(group[z], second)
-        add_group()
-        add_guest()
+            if c < len(between):
+                between[c]()
+        add_guest(far_end, 1)
         for c in chunks:
             part(0, c).wait_recv()
             grad_text[piece(c), :] = (
                 total[0, piece(c), :] + part_in[0, piece(c), :].astype(jnp.float32)
             )
 
-        part(1, CHUNKS - 1).wait_send()
+        for c in chunks[gate + 1 :]:
+            part(1, c).wait_send()
         for c in chunks:
             along(text, z, 0, far_middle, c).wait_send()
             along(text, z, 1, end, c).wait_send()
@@ -332,7 +355,8 @@
             row_block(c).wait_send()
 
     for slot in range(4):
-        across(text, slot).wait_send()
+        for c in chunks:
+            across(text, slot, c).wait_send()
 
 
 def solution(mesh):
@@ -353,7 +377,7 @@
                 pltpu.VMEM((2, *block), jnp.bfloat16),
                 pltpu.VMEM(block, jnp.bfloat16),
                 pltpu.VMEM(block, jnp.bfloat16),
-                dma((2,)), dma((4, 2, CHUNKS)), dma((4, CHUNKS)), dma((4,)), dma((4,)),
+                dma((2,)), dma((4, 2, CHUNKS)), dma((4, CHUNKS)), dma((4, CHUNKS)), dma((4, CHUNKS)),
                 dma((CHUNKS,)), dma((CHUNKS,)), dma((2, CHUNKS)), dma((2, CHUNKS)),
                 dma((2, CHUNKS)), dma((2, CHUNKS)), dma((CHUNKS,)), dma((CHUNKS,)),
             ]

time: 41.9 us -> 41 us (0.979)
  Pallas kernels: 38.2 us -> 37.3 us
    pallas_call x1, Pallas kernels: 38.2 us -> 37.3 us  [per_device(): pl.pallas_call(body, out_shape=(pltpu.VMEM((rows, width), jnp.float32),)...]
where the time goes in v7:
time: 41 us; the launch traced here: 40.8 us
  Pallas kernels  37.3 us (91%)
  between operations  1.93 us (5%)
  local copies, waits for them, and re-layouts  1.63 us (4%)
    pallas_call x1, Pallas kernels, per_device(): pl.pallas_call(body, out_shape=(pltpu.VMEM((rows, width), jnp.float32),)...  37.3 us
    unnamed x2, local copies, waits for them, and re-layouts  1.63 us

profile of v7, /device:TPU:0, one launch (start us, length us, event | category | flops | bytes accessed | tf_op | source)
XLA Modules:
  0.0 40.8 jit_solution(10308896231602568087)
XLA Ops:
  1.9 37.3 %shard_map.59 = (f32[128,1152]{1,0:T(8,128)S(1)}, f32[128,1152]{1,0:T(8,128)S(1)}) custom-call(bf16[128,1152]{1,0:T(8,128)(2,1)} %image.1, bf16[128,1152]{1,0:T(8,128)(2,1)} %text.1, f32[1]{0:T(128)S(6)} %copy.10.scale, f32[1]{0:T(128)S(6)} %copy.11.offset), custom_call_target="tpu_custom_call" | custom-call | flops 1207959552 | bytes 1769472 | tf_op jit(solution)/shard_map/pallas_call | solution.py:392
  39.2 0.8 %copy.8 = f32[128,1152]{1,0:T(8,128)} copy(f32[128,1152]{1,0:T(8,128)S(1)} %get-tuple-element.2) | data formatting | bytes 1179648
  40.0 0.8 %copy.9 = f32[128,1152]{1,0:T(8,128)} copy(f32[128,1152]{1,0:T(8,128)S(1)} %get-tuple-element.3) | data formatting | bytes 1179648

commit v8 on v7

--- a/solution.py
+++ b/solution.py
@@ -9,7 +9,8 @@
 
 MESH = pl.DeviceIdType.MESH
 TEXT, IMAGE = 0, 1
-CHUNKS = 4
+CHUNKS = 8
+AHEAD = 3
 
 
 def kernel(
@@ -133,7 +134,7 @@
 
 
 def line4_kernel(
-    m, image, text, scale, offset, grad_image, grad_text,
+    m, image, text, scale_in, offset_in, grad_image, grad_text, scale, offset,
     group, guest, images, total, part_out, part_in, row_out, row_in,
     load_sem, line_send, line_recv, side_send, side_recv, image_send, image_recv,
     guest_send, guest_recv, part_send, part_recv, row_send, row_recv,
@@ -151,6 +152,8 @@
     loads = [
         pltpu.make_async_copy(image, images.at[0], load_sem.at[0]),
         pltpu.make_async_copy(text, group.at[z], load_sem.at[1]),
+        pltpu.make_async_copy(scale_in, scale, load_sem.at[2]),
+        pltpu.make_async_copy(offset_in, offset, load_sem.at[3]),
     ]
     for load in loads:
         load.start()
@@ -303,7 +306,7 @@
         for c in chunks:
             image_across(image, 1, c).wait_recv()
         part_out[0] = (total[2] + pair(over[...], second)).astype(jnp.bfloat16)
-        for c in chunks[: CHUNKS // 2]:
+        for c in chunks[:AHEAD]:
             part(0, c).start()
         for c in chunks:
             along(text, far_end, 0, middle, c).wait_recv()
@@ -330,7 +333,7 @@
             if c == gate:
                 for early in chunks[: gate + 1]:
                     part(1, early).wait_send()
-                for late in chunks[CHUNKS // 2 :]:
+                for late in chunks[AHEAD:]:
                     part(0, late).start()
             if c < len(between):
                 between[c]()
@@ -369,6 +372,8 @@
         if n == 4:
             body = functools.partial(line4_kernel, m)
             scratch = [
+                pltpu.SMEM((1,), jnp.float32),
+                pltpu.SMEM((1,), jnp.float32),
                 pltpu.VMEM((4, *block), jnp.bfloat16),
                 pltpu.VMEM((4, *block), jnp.bfloat16),
                 pltpu.VMEM((4, *block), jnp.bfloat16),
@@ -377,7 +382,7 @@
                 pltpu.VMEM((2, *block), jnp.bfloat16),
                 pltpu.VMEM(block, jnp.bfloat16),
                 pltpu.VMEM(block, jnp.bfloat16),
-                dma((2,)), dma((4, 2, CHUNKS)), dma((4, CHUNKS)), dma((4, CHUNKS)), dma((4, CHUNKS)),
+                dma((4,)), dma((4, 2, CHUNKS)), dma((4, CHUNKS)), dma((4, CHUNKS)), dma((4, CHUNKS)),
                 dma((CHUNKS,)), dma((CHUNKS,)), dma((2, CHUNKS)), dma((2, CHUNKS)),
                 dma((2, CHUNKS)), dma((2, CHUNKS)), dma((CHUNKS,)), dma((CHUNKS,)),
             ]
@@ -393,7 +398,7 @@
             body,
             out_shape=(pltpu.VMEM((rows, width), jnp.float32),) * 2,
             in_specs=[pl.BlockSpec(memory_space=pltpu.HBM)] * 2
-            + [pl.BlockSpec(memory_space=pltpu.SMEM)] * 2,
+            + [pl.BlockSpec(memory_space=pltpu.HBM if n == 4 else pltpu.SMEM)] * 2,
             out_specs=(pl.BlockSpec(memory_space=pltpu.VMEM),) * 2,
             scratch_shapes=scratch,
             compiler_params=pltpu.CompilerParams(

time: 41 us -> 41.6 us (1.015)
  Pallas kernels: 37.3 us -> 37.9 us
    pallas_call x1, Pallas kernels: 37.3 us -> 37.9 us  [per_device(): pl.pallas_call(body, out_shape=(pltpu.VMEM((rows, width), jnp.float32),)...]
where the time goes in v8:
time: 41.6 us; the launch traced here: 41.5 us
  Pallas kernels  37.9 us (91%)
  between operations  1.93 us (5%)
  local copies, waits for them, and re-layouts  1.63 us (4%)
    pallas_call x1, Pallas kernels, per_device(): pl.pallas_call(body, out_shape=(pltpu.VMEM((rows, width), jnp.float32),)...  37.9 us
    unnamed x2, local copies, waits for them, and re-layouts  1.63 us

profile of v8, /device:TPU:0, one launch (start us, length us, event | category | flops | bytes accessed | tf_op | source)
XLA Modules:
  0.0 41.5 jit_solution(7152637454745435704)
XLA Ops:
  1.9 37.9 %shard_map.59 = (f32[128,1152]{1,0:T(8,128)S(1)}, f32[128,1152]{1,0:T(8,128)S(1)}) custom-call(bf16[128,1152]{1,0:T(8,128)(2,1)} %image.1, bf16[128,1152]{1,0:T(8,128)(2,1)} %text.1, f32[1]{0:T(128)S(6)} %copy.10.scale_in, f32[1]{0:T(128)S(6)} %copy.11.offset_in), custom_call_target="tpu_custom_call" | custom-call | flops 1207959552 | bytes 1769472 | tf_op jit(solution)/shard_map/pallas_call | solution.py:397
  39.8 0.8 %copy.8 = f32[128,1152]{1,0:T(8,128)} copy(f32[128,1152]{1,0:T(8,128)S(1)} %get-tuple-element.2) | data formatting | bytes 1179648
  40.6 0.8 %copy.9 = f32[128,1152]{1,0:T(8,128)} copy(f32[128,1152]{1,0:T(8,128)S(1)} %get-tuple-element.3) | data formatting | bytes 1179648

commit v9 on v7

--- a/solution.py
+++ b/solution.py
@@ -175,17 +175,24 @@
     def piece(c):
         return pl.ds(c * size, size)
 
+    def half(h):
+        return pl.ds(h * (rows // 2), rows // 2)
+
     def along(src, slot, way, to, c):
         return remote(
             src.at[piece(c)], group.at[slot, piece(c)],
             line_send.at[slot, way, c], line_recv.at[slot, c], outer, to,
         )
 
-    def across(src, slot, c):
-        return remote(
-            src.at[piece(c)], guest.at[slot, piece(c)],
-            side_send.at[slot, c], side_recv.at[slot, c], above, z,
-        )
+    def across(src, slot, h):
+        return remote(
+            src.at[half(h)], guest.at[slot, half(h)],
+            side_send.at[slot, h], side_recv.at[slot, h], above, z,
+        )
+
+    def across_after(src, slot, c):
+        if (c + 1) % (CHUNKS // 2) == 0:
+            across(src, slot, c // (CHUNKS // 2)).start()
 
     def image_inward(c):
         return remote(
@@ -199,15 +206,15 @@
             guest_send.at[i, c], guest_recv.at[i, c], below, z,
         )
 
-    def part(i, c):
-        return remote(
-            part_out.at[i, piece(c)], part_in.at[i, piece(c)],
-            part_send.at[i, c], part_recv.at[i, c], outer, far_middle,
-        )
-
-    def row_block(c):
-        return remote(
-            row_out.at[piece(c)], row_in.at[piece(c)], row_send.at[c], row_recv.at[c], outer, end
+    def part(i, h):
+        return remote(
+            part_out.at[i, half(h)], part_in.at[i, half(h)],
+            part_send.at[i, h], part_recv.at[i, h], outer, far_middle,
+        )
+
+    def row_block(h):
+        return remote(
+            row_out.at[half(h)], row_in.at[half(h)], row_send.at[h], row_recv.at[h], outer, end
         )
 
     def weigh(left, right, match=None):
@@ -235,8 +242,8 @@
 
     def add_guest(slot, count):
         for k in range(count):
-            for c in chunks:
-                across(text, slot + k, c).wait_recv()
+            for h in (0, 1):
+                across(text, slot + k, h).wait_recv()
         grad_image[...] += pair(images[0], guest.at[pl.ds(slot, count)])
 
     chunks = range(CHUNKS)
@@ -245,8 +252,8 @@
     def _():
         for c in chunks:
             image_inward(c).start()
-        for c in chunks:
-            across(text, z, c).start()
+        for h in (0, 1):
+            across(text, z, h).start()
         for load in loads:
             load.wait()
         for c in chunks[:-1]:
@@ -257,15 +264,15 @@
         for slot in (middle, far_middle, far_end):
             for c in chunks:
                 along(text, slot, 0, end, c).wait_recv()
-                across(group.at[slot], slot, c).start()
+                across_after(group.at[slot], slot, c)
         add_group(1, 2)
         add_group(far_end, 1)
         add_guest(end, 1)
         add_guest(1, 2)
         add_guest(far_end, 1)
-        for c in chunks:
-            row_block(c).wait_recv()
-            grad_text[piece(c), :] = row_in[piece(c), :].astype(jnp.float32)
+        for h in (0, 1):
+            row_block(h).wait_recv()
+            grad_text[half(h), :] = row_in[half(h), :].astype(jnp.float32)
         image_inward(CHUNKS - 1).wait_send()
         for c in chunks:
             along(text, z, 0, middle, c).wait_send()
@@ -279,8 +286,8 @@
             along(text, z, 1, end, c).start()
         for c in chunks:
             image_across(image, 0, c).start()
-        for c in chunks:
-            across(text, z, c).start()
+        for h in (0, 1):
+            across(text, z, h).start()
         for load in loads:
             load.wait()
         for c in chunks:
@@ -288,14 +295,14 @@
             image_across(images.at[2], 1, c).start()
             along(text, far_middle, 0, middle, c).wait_recv()
             along(over, far_middle, 0, end, c).start()
-            across(over, far_middle, c).start()
+            across_after(over, far_middle, c)
         for c in chunks:
             image_across(image, 0, c).wait_recv()
         total[2] = pair(over[...], first)
         for c in chunks:
             along(text, end, 0, middle, c).wait_recv()
             along(beside, end, 0, far_middle, c).start()
-            across(beside, end, c).start()
+            across_after(beside, end, c)
             if c == 0:
                 total[0] = pair(group[z], first, 0)
             if c == 1:
@@ -303,46 +310,40 @@
         for c in chunks:
             image_across(image, 1, c).wait_recv()
         part_out[0] = (total[2] + pair(over[...], second)).astype(jnp.bfloat16)
-        for c in chunks[: CHUNKS // 2]:
-            part(0, c).start()
+        part(0, 0).start()
         for c in chunks:
             along(text, far_end, 0, middle, c).wait_recv()
             along(far, far_end, 0, end, c).start()
-            across(far, far_end, c).start()
+            across_after(far, far_end, c)
         part_out[1] = pair(far[...], images).astype(jnp.bfloat16)
-        for c in chunks:
-            part(1, c).start()
+        for h in (0, 1):
+            part(1, h).start()
         total[1] = pair(beside[...], images, 2 * rows)
         total[0] += pair(group[z], second)
-        between = (
-            lambda: add_group(end, 1),
-            lambda: add_group(far_end, 1),
-            lambda: add_guest(1, 2),
-            lambda: add_guest(end, 1),
-        )
-        gate = CHUNKS // 2 - 1
-        for c in chunks:
-            part(1, c).wait_recv()
-            row_out[piece(c), :] = (
-                total[1, piece(c), :] + part_in[1, piece(c), :].astype(jnp.float32)
+        for h in (0, 1):
+            part(1, h).wait_recv()
+            row_out[half(h), :] = (
+                total[1, half(h), :] + part_in[1, half(h), :].astype(jnp.float32)
             ).astype(jnp.bfloat16)
-            row_block(c).start()
-            if c == gate:
-                for early in chunks[: gate + 1]:
-                    part(1, early).wait_send()
-                for late in chunks[CHUNKS // 2 :]:
-                    part(0, late).start()
-            if c < len(between):
-                between[c]()
+            row_block(h).start()
+            if h == 0:
+                part(1, 0).wait_send()
+                part(0, 1).start()
+                add_group(end, 1)
+                add_group(far_end, 1)
+        add_guest(1, 2)
+        add_guest(end, 1)
         add_guest(far_end, 1)
-        for c in chunks:
-            part(0, c).wait_recv()
-            grad_text[piece(c), :] = (
-                total[0, piece(c), :] + part_in[0, piece(c), :].astype(jnp.float32)
+        for h in (0, 1):
+            part(0, h).wait_recv()
+            grad_text[half(h), :] = (
+                total[0, half(h), :] + part_in[0, half(h), :].astype(jnp.float32)
             )
 
-        for c in chunks[gate + 1 :]:
-            part(1, c).wait_send()
+        part(1, 1).wait_send()
+        for h in (0, 1):
+            part(0, h).wait_send()
+            row_block(h).wait_send()
         for c in chunks:
             along(text, z, 0, far_middle, c).wait_send()
             along(text, z, 1, end, c).wait_send()
@@ -351,12 +352,10 @@
             along(text, far_end, 0, end, c).wait_send()
             image_across(image, 0, c).wait_send()
             image_across(image, 1, c).wait_send()
-            part(0, c).wait_send()
-            row_block(c).wait_send()
 
     for slot in range(4):
-        for c in chunks:
-            across(text, slot, c).wait_send()
+        for h in (0, 1):
+            across(text, slot, h).wait_send()
 
 
 def solution(mesh):
@@ -377,9 +376,9 @@
                 pltpu.VMEM((2, *block), jnp.bfloat16),
                 pltpu.VMEM(block, jnp.bfloat16),
                 pltpu.VMEM(block, jnp.bfloat16),
-                dma((2,)), dma((4, 2, CHUNKS)), dma((4, CHUNKS)), dma((4, CHUNKS)), dma((4, CHUNKS)),
+                dma((2,)), dma((4, 2, CHUNKS)), dma((4, CHUNKS)), dma((4, 2)), dma((4, 2)),
                 dma((CHUNKS,)), dma((CHUNKS,)), dma((2, CHUNKS)), dma((2, CHUNKS)),
-                dma((2, CHUNKS)), dma((2, CHUNKS)), dma((CHUNKS,)), dma((CHUNKS,)),
+                dma((2, 2)), dma((2, 2)), dma((2,)), dma((2,)),
             ]
         else:
             body = functools.partial(kernel, n, m)

time: 41 us -> 42.1 us (1.027)
  Pallas kernels: 37.3 us -> 38.4 us
    pallas_call x1, Pallas kernels: 37.3 us -> 38.4 us  [per_device(): pl.pallas_call(body, out_shape=(pltpu.VMEM((rows, width), jnp.float32),)...]
where the time goes in v9:
time: 42.1 us; the launch traced here: 41.9 us
  Pallas kernels  38.4 us (91%)
  between operations  1.93 us (5%)
  local copies, waits for them, and re-layouts  1.63 us (4%)
    pallas_call x1, Pallas kernels, per_device(): pl.pallas_call(body, out_shape=(pltpu.VMEM((rows, width), jnp.float32),)...  38.4 us
    unnamed x2, local copies, waits for them, and re-layouts  1.63 us

profile of v9, /device:TPU:0, one launch (start us, length us, event | category | flops | bytes accessed | tf_op | source)
XLA Modules:
  0.0 41.9 jit_solution(6005497950528591635)
XLA Ops:
  1.9 38.4 %shard_map.59 = (f32[128,1152]{1,0:T(8,128)S(1)}, f32[128,1152]{1,0:T(8,128)S(1)}) custom-call(bf16[128,1152]{1,0:T(8,128)(2,1)} %image.1, bf16[128,1152]{1,0:T(8,128)(2,1)} %text.1, f32[1]{0:T(128)S(6)} %copy.10.scale, f32[1]{0:T(128)S(6)} %copy.11.offset), custom_call_target="tpu_custom_call" | custom-call | flops 1207959552 | bytes 1769472 | tf_op jit(solution)/shard_map/pallas_call | solution.py:391
  40.3 0.8 %copy.8 = f32[128,1152]{1,0:T(8,128)} copy(f32[128,1152]{1,0:T(8,128)S(1)} %get-tuple-element.2) | data formatting | bytes 1179648
  41.1 0.8 %copy.9 = f32[128,1152]{1,0:T(8,128)} copy(f32[128,1152]{1,0:T(8,128)S(1)} %get-tuple-element.3) | data formatting | bytes 1179648

commit v10 on v7

--- a/solution.py
+++ b/solution.py
@@ -136,7 +136,7 @@
     m, image, text, scale, offset, grad_image, grad_text,
     group, guest, images, total, part_out, part_in, row_out, row_in,
     load_sem, line_send, line_recv, side_send, side_recv, image_send, image_recv,
-    guest_send, guest_recv, part_send, part_recv, row_send, row_recv,
+    guest_send, guest_recv, part_send, part_recv, row_send, row_recv, turn,
 ):
     outer, z = lax.axis_index("outer"), lax.axis_index("inner")
     above, below = lax.rem(outer + 1, m), lax.rem(outer + m - 1, m)
@@ -244,15 +244,24 @@
     @pl.when(is_end)
     def _():
         for c in chunks:
+            along(text, z, 0, middle, c).start()
+        for c in chunks:
+            across(text, z, c).start()
+        for c in chunks[:-1]:
+            along(text, z, 0, middle, c).wait_send()
+        odd = lax.rem(outer, 2) == 1
+        pl.when(odd)(lambda: pl.semaphore_wait(turn, 1))
+        for c in chunks:
             image_inward(c).start()
-        for c in chunks:
-            across(text, z, c).start()
+        for c in chunks[:-1]:
+            image_inward(c).wait_send()
+        pl.when(jnp.logical_not(odd) & (outer + 1 < m))(
+            lambda: pl.semaphore_signal(
+                turn, inc=1, device_id=(above, z), device_id_type=MESH
+            )
+        )
         for load in loads:
             load.wait()
-        for c in chunks[:-1]:
-            image_inward(c).wait_send()
-        for c in chunks:
-            along(text, z, 0, middle, c).start()
         add_group(z, 1, 0, first=True)
         for slot in (middle, far_middle, far_end):
             for c in chunks:
@@ -267,8 +276,7 @@
             row_block(c).wait_recv()
             grad_text[piece(c), :] = row_in[piece(c), :].astype(jnp.float32)
         image_inward(CHUNKS - 1).wait_send()
-        for c in chunks:
-            along(text, z, 0, middle, c).wait_send()
+        along(text, z, 0, middle, CHUNKS - 1).wait_send()
 
     @pl.when(is_middle)
     def _():
@@ -284,43 +292,41 @@
         for load in loads:
             load.wait()
         for c in chunks:
-            image_inward(c).wait_recv()
-            image_across(images.at[2], 1, c).start()
+            along(text, end, 0, middle, c).wait_recv()
+            along(beside, end, 0, far_middle, c).start()
+            across(beside, end, c).start()
+        for c in chunks:
             along(text, far_middle, 0, middle, c).wait_recv()
             along(over, far_middle, 0, end, c).start()
             across(over, far_middle, c).start()
         for c in chunks:
             image_across(image, 0, c).wait_recv()
         total[2] = pair(over[...], first)
-        for c in chunks:
-            along(text, end, 0, middle, c).wait_recv()
-            along(beside, end, 0, far_middle, c).start()
-            across(beside, end, c).start()
+        total[1] = pair(beside[...], first)
+        for c in chunks:
+            image_inward(c).wait_recv()
+            image_across(images.at[2], 1, c).start()
             if c == 0:
                 total[0] = pair(group[z], first, 0)
-            if c == 1:
-                add_group(1, 2, (z - 1) * rows, first=True)
-        for c in chunks:
-            image_across(image, 1, c).wait_recv()
-        part_out[0] = (total[2] + pair(over[...], second)).astype(jnp.bfloat16)
-        for c in chunks[: CHUNKS // 2]:
-            part(0, c).start()
         for c in chunks:
             along(text, far_end, 0, middle, c).wait_recv()
             along(far, far_end, 0, end, c).start()
             across(far, far_end, c).start()
+        for c in chunks:
+            image_across(image, 1, c).wait_recv()
         part_out[1] = pair(far[...], images).astype(jnp.bfloat16)
         for c in chunks:
             part(1, c).start()
-        total[1] = pair(beside[...], images, 2 * rows)
+        part_out[0] = (total[2] + pair(over[...], second)).astype(jnp.bfloat16)
+        total[1] += pair(beside[...], second, 0)
         total[0] += pair(group[z], second)
         between = (
+            lambda: add_group(1, 2, (z - 1) * rows, first=True),
             lambda: add_group(end, 1),
             lambda: add_group(far_end, 1),
             lambda: add_guest(1, 2),
-            lambda: add_guest(end, 1),
-        )
-        gate = CHUNKS // 2 - 1
+        )
+        gate = CHUNKS - 2
         for c in chunks:
             part(1, c).wait_recv()
             row_out[piece(c), :] = (
@@ -330,10 +336,11 @@
             if c == gate:
                 for early in chunks[: gate + 1]:
                     part(1, early).wait_send()
-                for late in chunks[CHUNKS // 2 :]:
+                for late in chunks:
                     part(0, late).start()
             if c < len(between):
                 between[c]()
+        add_guest(end, 1)
         add_guest(far_end, 1)
         for c in chunks:
             part(0, c).wait_recv()
@@ -380,6 +387,7 @@
                 dma((2,)), dma((4, 2, CHUNKS)), dma((4, CHUNKS)), dma((4, CHUNKS)), dma((4, CHUNKS)),
                 dma((CHUNKS,)), dma((CHUNKS,)), dma((2, CHUNKS)), dma((2, CHUNKS)),
                 dma((2, CHUNKS)), dma((2, CHUNKS)), dma((CHUNKS,)), dma((CHUNKS,)),
+                pltpu.SemaphoreType.REGULAR,
             ]
         else:
             body = functools.partial(kernel, n, m)

time: 41 us -> 40.4 us (0.985)
  the two profiles are of different devices: /device:TPU:0 before, /device:TPU:9 now
where the time goes in v10:
time: 40.4 us; the launch traced here: 40.3 us
  Pallas kernels  36.7 us (91%)
  between operations  1.93 us (5%)
  local copies, waits for them, and re-layouts  1.63 us (4%)
    pallas_call x1, Pallas kernels, per_device(): pl.pallas_call(body, out_shape=(pltpu.VMEM((rows, width), jnp.float32),)...  36.7 us
    unnamed x2, local copies, waits for them, and re-layouts  1.63 us

profile of v10, /device:TPU:9, one launch (start us, length us, event | category | flops | bytes accessed | tf_op | source)
XLA Modules:
  0.0 40.3 jit_solution(4845715607740960861)
XLA Ops:
  1.9 36.7 %shard_map.59 = (f32[128,1152]{1,0:T(8,128)S(1)}, f32[128,1152]{1,0:T(8,128)S(1)}) custom-call(bf16[128,1152]{1,0:T(8,128)(2,1)} %image.1, bf16[128,1152]{1,0:T(8,128)(2,1)} %text.1, f32[1]{0:T(128)S(6)} %copy.10.scale, f32[1]{0:T(128)S(6)} %copy.11.offset), custom_call_target="tpu_custom_call" | custom-call | flops 1207959552 | bytes 1769472 | tf_op jit(solution)/shard_map/pallas_call | solution.py:400
  38.7 0.8 %copy.8 = f32[128,1152]{1,0:T(8,128)} copy(f32[128,1152]{1,0:T(8,128)S(1)} %get-tuple-element.2) | data formatting | bytes 1179648
  39.5 0.8 %copy.9 = f32[128,1152]{1,0:T(8,128)} copy(f32[128,1152]{1,0:T(8,128)S(1)} %get-tuple-element.3) | data formatting | bytes 1179648

commit v11 on v10

--- a/solution.py
+++ b/solution.py
@@ -326,7 +326,7 @@
             lambda: add_group(far_end, 1),
             lambda: add_guest(1, 2),
         )
-        gate = CHUNKS - 2
+        gate = 0
         for c in chunks:
             part(1, c).wait_recv()
             row_out[piece(c), :] = (

time: 40.4 us -> 40.4 us (level)
  no operation moved by 1% of the time
where the time goes in v11:
time: 40.4 us; the launch traced here: 40.3 us
  Pallas kernels  36.7 us (91%)
  between operations  1.93 us (5%)
  local copies, waits for them, and re-layouts  1.63 us (4%)
    pallas_call x1, Pallas kernels, per_device(): pl.pallas_call(body, out_shape=(pltpu.VMEM((rows, width), jnp.float32),)...  36.7 us
    unnamed x2, local copies, waits for them, and re-layouts  1.63 us

profile of v11, /device:TPU:9, one launch (start us, length us, event | category | flops | bytes accessed | tf_op | source)
XLA Modules:
  0.0 40.3 jit_solution(10842317941368405528)
XLA Ops:
  1.9 36.7 %shard_map.59 = (f32[128,1152]{1,0:T(8,128)S(1)}, f32[128,1152]{1,0:T(8,128)S(1)}) custom-call(bf16[128,1152]{1,0:T(8,128)(2,1)} %image.1, bf16[128,1152]{1,0:T(8,128)(2,1)} %text.1, f32[1]{0:T(128)S(6)} %copy.10.scale, f32[1]{0:T(128)S(6)} %copy.11.offset), custom_call_target="tpu_custom_call" | custom-call | flops 1207959552 | bytes 1769472 | tf_op jit(solution)/shard_map/pallas_call | solution.py:400
  38.7 0.8 %copy.8 = f32[128,1152]{1,0:T(8,128)} copy(f32[128,1152]{1,0:T(8,128)S(1)} %get-tuple-element.2) | data formatting | bytes 1179648
  39.5 0.8 %copy.9 = f32[128,1152]{1,0:T(8,128)} copy(f32[128,1152]{1,0:T(8,128)S(1)} %get-tuple-element.3) | data formatting | bytes 1179648
